TPU v7x, 32 devices: a whole 2x2x4 slice. The times are simulated.
32 devices in a mesh: blk: 32 (over z, y, x, core).
Axes of the slice: x: 2, y: 2, z: 4, core: 2. Of those that a mesh axis runs over, the one named last changes fastest.
Arguments:
- query_states: bfloat16 [8192, 4096], P('blk'), may hold values from -6 to 6
- rotated_key_state: bfloat16 [8192, 1024], P('blk'), may hold values from -6 to 6
- value_state_rows: bfloat16 [8192, 1024], P('blk'), may hold values from -6 to 6
- positions: int32 [8192], P('blk'), may hold values from 0 to 1535, as said below
- residual: bfloat16 [8192, 4096], P('blk'), may hold values from -6 to 6
- norm_gain: float32 [4096], replicated, may hold values from 0.1 to 1.9
- gate_weight: bfloat16 [14336, 4096], P('blk'), may hold values from -0.09375 to 0.09375
- up_weight: bfloat16 [14336, 4096], P('blk'), may hold values from -0.09375 to 0.09375
- down_weight: bfloat16 [14336, 4096], P('blk'), may hold values from -0.125 to 0.125
Outputs:
- attended: bfloat16 [8192, 4096], P('blk')
- ffn_part: bfloat16 [8192, 4096], P('blk')
Inputs may be any that keep to these rules, and one draw needn't show every extreme that they name: positions[0] is 0 and every later entry is 0 or one more than the entry before it.
All inputs are finite; a program needn't handle non-finite values.
Results may differ from a plain program's by a relative error of at most 0.0065.
Values may be sent and summed in bfloat16 or wider, within the bound.
A program may use at most 128 MiB of HBM per device.

v0:
```python
import math

import jax
import jax.numpy as jnp
from jax import lax
from jax.sharding import PartitionSpec as P

QUERY_HEADS = 32
KEY_VALUE_HEADS = 8
HEAD_SIZE = 128
WINDOW_BLOCKS = 4
FFN_STEPS = 4


def passed_along(value, axis, by):
    length = lax.axis_size(axis)
    pairs = [(i, i + by) for i in range(length) if 0 <= i + by < length]
    return lax.ppermute(value, axis, pairs)


def shifted(value, axis, steps):
    count = lax.axis_size(axis)
    pairs = [(source, (source + steps) % count) for source in range(count)]
    return lax.ppermute(value, axis, pairs)


def shard_term(rows_in, gate_rows, up_rows, down_rows):
    contract = (((1,), (1,)), ((), ()))
    gate_value = lax.dot_general(rows_in, gate_rows, contract, preferred_element_type=jnp.float32)
    up_value = lax.dot_general(rows_in, up_rows, contract, preferred_element_type=jnp.float32)
    hidden = (jax.nn.silu(gate_value) * up_value).astype(jnp.bfloat16)
    return jnp.dot(hidden, down_rows, preferred_element_type=jnp.float32)


def per_device(
    query_states,
    rotated_key_state,
    value_state_rows,
    positions,
    residual,
    norm_gain,
    gate_weight,
    up_weight,
    down_weight,
):
    block_rows = query_states.shape[0]
    device_index = lax.axis_index("blk")
    heads_per_group = QUERY_HEADS // KEY_VALUE_HEADS
    arrived = [(rotated_key_state, value_state_rows)]
    for offset in range(1, WINDOW_BLOCKS):
        arrived.append(passed_along((rotated_key_state, value_state_rows), "blk", offset))
    ordered = arrived[::-1]
    key_window = jnp.concatenate([block_pair[0] for block_pair in ordered], axis=0)
    value_window = jnp.concatenate([block_pair[1] for block_pair in ordered], axis=0)
    query_index = device_index * block_rows + jnp.arange(block_rows, dtype=jnp.int32)
    key_index = (device_index - (WINDOW_BLOCKS - 1)) * block_rows + jnp.arange(
        WINDOW_BLOCKS * block_rows, dtype=jnp.int32
    )
    visible = (key_index[None, :] <= query_index[:, None]) & (
        key_index[None, :] >= (query_index - positions)[:, None]
    )
    score_scale = 1.0 / math.sqrt(HEAD_SIZE)

    def group_of_head(group_index, attended_rows):
        query_block = lax.dynamic_slice_in_dim(
            query_states, group_index * heads_per_group * HEAD_SIZE, heads_per_group * HEAD_SIZE, 1
        )
        query_block = query_block.reshape(block_rows, heads_per_group, HEAD_SIZE)
        key_block = lax.dynamic_slice_in_dim(key_window, group_index * HEAD_SIZE, HEAD_SIZE, 1)
        value_block = lax.dynamic_slice_in_dim(value_window, group_index * HEAD_SIZE, HEAD_SIZE, 1)
        scores = (
            jnp.einsum("trd,kd->rtk", query_block, key_block, preferred_element_type=jnp.float32)
            * score_scale
        )
        scores = jnp.where(visible[None], scores, -jnp.inf)
        row_max = jnp.max(scores, axis=-1, keepdims=True)
        weights = jnp.exp(scores - row_max)
        denominator = jnp.sum(weights, axis=-1, keepdims=True)
        mixed = (
            jnp.einsum(
                "rtk,kd->rtd",
                weights.astype(jnp.bfloat16),
                value_block,
                preferred_element_type=jnp.float32,
            )
            / denominator
        )
        result = (
            jnp.transpose(mixed, (1, 0, 2))
            .reshape(block_rows, heads_per_group * HEAD_SIZE)
            .astype(jnp.bfloat16)
        )
        return lax.dynamic_update_slice_in_dim(
            attended_rows, result, group_index * heads_per_group * HEAD_SIZE, 1
        )

    attended = lax.fori_loop(
        0,
        KEY_VALUE_HEADS,
        group_of_head,
        jnp.zeros((block_rows, QUERY_HEADS * HEAD_SIZE), jnp.bfloat16),
    )
    stream = residual.astype(jnp.float32) + attended.astype(jnp.float32)
    normed = (
        stream * lax.rsqrt(jnp.mean(stream * stream, axis=-1, keepdims=True) + 1e-05) * norm_gain
    ).astype(jnp.bfloat16)
    ffn_total = shard_term(normed, gate_weight, up_weight, down_weight)
    current_weights = (gate_weight, up_weight, down_weight)
    for offset in range(1, FFN_STEPS):
        current_weights = shifted(
            (current_weights[0], current_weights[1], current_weights[2]), "blk", -1
        )
        ffn_total = ffn_total + shard_term(
            normed, current_weights[0], current_weights[1], current_weights[2]
        )
    return (attended, ffn_total.astype(jnp.bfloat16))


def solution(mesh):
    in_specs = (
        P("blk", None),
        P("blk", None),
        P("blk", None),
        P("blk"),
        P("blk", None),
        P(),
        P("blk", None),
        P("blk", None),
        P("blk", None),
    )
    out_specs = (P("blk", None), P("blk", None))
    return jax.shard_map(
        per_device, mesh=mesh, in_specs=in_specs, out_specs=out_specs, check_vma=False
    )
```

profile of v0, /device:TPU:19, one launch (start us, length us, event | category | flops | bytes accessed | tf_op | source)
XLA Modules:
  0.0 431.9 jit_solution(12219507204453920667)
XLA Ops:
  3.3 3.9 collective-permute-start.3
  7.2 4.1 collective-permute-start.4
  11.3 123.6 %collective-permute-done.3 = bf16[256,1024]{0,1:T(8,128)(2,1)S(1)} collective-permute-done((bf16[256,1024]{0,1:T(8,128)(2,1)S(1)}, bf16[256,1024]{0,1:T(8,128)(2,1)S(1)}, u32[]{:S(2)}, u32[]{:S(2)}) %collective-permute-start.3) | collective-permute-done | bytes 524320 | tf_op jit(solution)/shard_map/ppermute | solution.py:18
  136.8 10.1 %collective-permute-start = (bf16[256,1024]{1,0:T(8,128)(2,1)}, bf16[256,1024]{1,0:T(8,128)(2,1)S(1)}, u32[]{:S(2)}, u32[]{:S(2)}) collective-permute-start(bf16[256,1024]{1,0:T(8,128)(2,1)} %param.12), channel_id=1, source_target_pairs={{0,3},{1,4},{2,5},{3,6},{4,7},{5,8},{6,9},{7,10},{8,11},{9,12},{10... | collective-permute-start | bytes 1572872 | tf_op jit(solution)/shard_map/ppermute | solution.py:18
  147.0 4.1 copy.25
  151.1 6.8 %collective-permute-start.1 = (bf16[256,1024]{1,0:T(8,128)(2,1)S(1)}, bf16[256,1024]{1,0:T(8,128)(2,1)S(1)}, u32[]{:S(2)}, u32[]{:S(2)}) collective-permute-start(bf16[256,1024]{1,0:T(8,128)(2,1)S(1)} %copy-done.2), channel_id=1, source_target_pairs={{0,2},{1,3},{2,4},{3,5},{4,6},{5,7},{6,8},{7,9},{8,10},{9,11},{10,... | collective-permute-start | bytes 1572872 | tf_op jit(solution)/shard_map/ppermute | solution.py:18
  157.9 15.6 %collective-permute-start.2 = (bf16[256,1024]{1,0:T(8,128)(2,1)S(1)}, bf16[256,1024]{1,0:T(8,128)(2,1)S(1)}, u32[]{:S(2)}, u32[]{:S(2)}) collective-permute-start(bf16[256,1024]{1,0:T(8,128)(2,1)S(1)} %copy-done.2), channel_id=1, source_target_pairs={{0,1},{1,2},{2,3},{3,4},{4,5},{5,6},{6,7},{7,8},{8,9},{9,10},{10,1... | collective-permute-start | bytes 1572872 | tf_op jit(solution)/shard_map/ppermute | solution.py:18
  175.1 4.5 %collective-permute-done.2 = bf16[256,1024]{1,0:T(8,128)(2,1)S(1)} collective-permute-done((bf16[256,1024]{1,0:T(8,128)(2,1)S(1)}, bf16[256,1024]{1,0:T(8,128)(2,1)S(1)}, u32[]{:S(2)}, u32[]{:S(2)}) %collective-permute-start.2) | collective-permute-done | bytes 524320 | tf_op jit(solution)/shard_map/ppermute | solution.py:18
  181.4 50.2 %while.16 = (s32[]{:T(128)}, bf16[256,4096]{0,1:T(8,128)(2,1)S(1)}, bf16[1024,1024]{1,0:T(8,128)(2,1)}, bf16[256,4096]{1,0:T(8,128)(2,1)}, bf16[1024,1024]{0,1:T...) while((s32[]{:T(128)}, bf16[256,4096]{0,1:T(8,128)(2,1)S(1)}, ...), condition=%wide.region_3.4_spmd.clone, body=%wide.region_0.3_spmd.clone.sunk | while | flops 549451776 | bytes 16279793 | solution.py:97
  185.5 2.2 fusion.85
  191.7 2.2 fusion.85
  198.0 2.2 fusion.85
  204.3 2.2 fusion.85
  210.5 2.2 fusion.85
  216.8 2.2 fusion.85
  223.1 2.2 fusion.85
  229.4 2.2 fusion.85
  231.6 2.9 copy.26
  234.5 2.5 multiply_reduce_fusion
  237.0 2.2 multiply_convert_fusion
  240.8 23.9 %collective-permute-done.10 = bf16[448,4096]{1,0:T(8,128)(2,1)} collective-permute-done((bf16[448,4096]{1,0:T(8,128)(2,1)}, bf16[448,4096]{1,0:T(8,128)(2,1)}, u32[]{:S(2)}, u32[]{:S(2)}) %collective-permute-start.10) | collective-permute-done | bytes 3670048 | tf_op jit(solution)/shard_map/ppermute | solution.py:24
  264.7 39.3 %collective-permute-done.11 = bf16[448,4096]{1,0:T(8,128)(2,1)} collective-permute-done((bf16[448,4096]{1,0:T(8,128)(2,1)}, bf16[448,4096]{1,0:T(8,128)(2,1)}, u32[]{:S(2)}, u32[]{:S(2)}) %collective-permute-start.11) | collective-permute-done | bytes 3670048 | tf_op jit(solution)/shard_map/ppermute | solution.py:24
  304.0 9.3 %fusion.28 = f32[256,4096]{1,0:T(8,128)} fusion(bf16[448,4096]{1,0:T(8,128)(2,1)} %param.19, bf16[448,4096]{1,0:T(8,128)(2,1)} %param.18, bf16[256,4096]{0,1:T(8,128)(2,1)S(1)} %multiply_convert_fusion, f32[256,448]{0,1:T(8,128)S(1)} %fusion.49), kind=kOutput, calls=%fused_computation.34 | convolution fusion | flops 1879736320 | bytes 14090240 | tf_op jit(solution)/shard_map/dot_general | solution.py:32
  313.3 3.1 fusion.50
  316.5 10.5 %convolution_add_fusion.2 = f32[256,4096]{1,0:T(8,128)} fusion(f32[256,4096]{1,0:T(8,128)} %fusion.28, bf16[448,4096]{1,0:T(8,128)(2,1)} %collective-permute-done.8, f32[256,448]{0,1:T(8,128)S(1)} %fusion.50, bf16[448,4096]{1,0:T(8,128)(2,1)} %collective-permute-done.7, bf16[256,4096]{0,1:T(8,128)(2,1)S(1)} %multiply_convert_fusion), kind=kOutput, calls=%fused_computation.25 | convolution fusion | flops 1880784896 | bytes 18284544 | tf_op jit(solution)/shard_map/dot_general | solution.py:32
  327.0 3.1 fusion.51
  330.2 10.5 %convolution_add_fusion.1 = f32[256,4096]{1,0:T(8,128)} fusion(f32[256,4096]{1,0:T(8,128)} %convolution_add_fusion.2, bf16[448,4096]{1,0:T(8,128)(2,1)} %collective-permute-done.11, f32[256,448]{0,1:T(8,128)S(1)} %fusion.51, bf16[448,4096]{1,0:T(8,128)(2,1)} %collective-permute-done.10, bf16[256,4096]{0,1:T(8,128)(2,1)S(1)} %multiply_convert_fusion), kind=kOutput, calls=%fused_computation.24 | convolution fusion | flops 1880784896 | bytes 18284544 | tf_op jit(solution)/shard_map/dot_general | solution.py:32
  340.7 2.6 collective-permute-done.12
  343.3 3.4 fusion.52
  346.7 35.9 %collective-permute-done.13 = bf16[448,4096]{1,0:T(8,128)(2,1)} collective-permute-done((bf16[448,4096]{1,0:T(8,128)(2,1)}, bf16[448,4096]{1,0:T(8,128)(2,1)}, u32[]{:S(2)}, u32[]{:S(2)}) %collective-permute-start.13) | collective-permute-done | bytes 3670048 | tf_op jit(solution)/shard_map/ppermute | solution.py:24
  382.6 39.3 %collective-permute-done.14 = bf16[448,4096]{1,0:T(8,128)(2,1)} collective-permute-done((bf16[448,4096]{1,0:T(8,128)(2,1)}, bf16[448,4096]{1,0:T(8,128)(2,1)}, u32[]{:S(2)}, u32[]{:S(2)}) %collective-permute-start.14) | collective-permute-done | bytes 3670048 | tf_op jit(solution)/shard_map/ppermute | solution.py:24
  422.0 9.9 %fusion.26 = bf16[256,4096]{1,0:T(8,128)(2,1)} fusion(f32[256,4096]{1,0:T(8,128)} %convolution_add_fusion.1, bf16[448,4096]{1,0:T(8,128)(2,1)} %collective-permute-done.14, f32[256,448]{0,1:T(8,128)S(1)} %fusion.52, bf16[448,4096]{1,0:T(8,128)(2,1)} %collective-permute-done.13, bf16[256,4096]{0,1:T(8,128)(2,1)S(1)} %multiply_convert_fusion), kind=kOutput, calls=%fused_computation.26 | convolution fusion | flops 1881833472 | bytes 16187392 | tf_op jit(solution)/shard_map/dot_general | solution.py:32
  (86 shorter events, 41.9 us)
Async XLA Ops:
  0.6 150.4 %copy-start.2 = (bf16[256,1024]{1,0:T(8,128)(2,1)S(1)}, bf16[256,1024]{1,0:T(8,128)(2,1)}, u32[]{:S(2)}) copy-start(bf16[256,1024]{1,0:T(8,128)(2,1)} %param.12) | copy-start | bytes 1572868
  0.6 172.9 %copy-start.4 = (s32[256]{0:T(256)S(1)}, s32[256]{0:T(256)}, u32[]{:S(2)}) copy-start(s32[256]{0:T(256)} %param.14) | copy-start | bytes 3076
  0.7 180.4 %collective-permute-start.6 = (bf16[448,4096]{1,0:T(8,128)(2,1)}, bf16[448,4096]{1,0:T(8,128)(2,1)}, u32[]{:S(2)}, u32[]{:S(2)}) collective-permute-start(bf16[448,4096]{1,0:T(8,128)(2,1)} %param.17), channel_id=1, source_target_pairs={{0,31},{1,0},{2,1},{3,2},{4,3},{5,4},{6,5},{7,6},{8,7},{9,8},{10,9... | collective-permute-start | bytes 11010056 | tf_op jit(solution)/shard_map/ppermute | solution.py:24
  1.4 179.7 %collective-permute-start.7 = (bf16[448,4096]{1,0:T(8,128)(2,1)}, bf16[448,4096]{1,0:T(8,128)(2,1)}, u32[]{:S(2)}, u32[]{:S(2)}) collective-permute-start(bf16[448,4096]{1,0:T(8,128)(2,1)} %param.18), channel_id=1, source_target_pairs={{0,31},{1,0},{2,1},{3,2},{4,3},{5,4},{6,5},{7,6},{8,7},{9,8},{10,9... | collective-permute-start | bytes 11010056 | tf_op jit(solution)/shard_map/ppermute | solution.py:24
  1.4 179.7 %collective-permute-start.8 = (bf16[448,4096]{1,0:T(8,128)(2,1)}, bf16[448,4096]{1,0:T(8,128)(2,1)}, u32[]{:S(2)}, u32[]{:S(2)}) collective-permute-start(bf16[448,4096]{1,0:T(8,128)(2,1)} %param.19), channel_id=1, source_target_pairs={{0,31},{1,0},{2,1},{3,2},{4,3},{5,4},{6,5},{7,6},{8,7},{9,8},{10,9... | collective-permute-start | bytes 11010056 | tf_op jit(solution)/shard_map/ppermute | solution.py:24
  3.3 131.6 %collective-permute-start.3 = (bf16[256,1024]{0,1:T(8,128)(2,1)S(1)}, bf16[256,1024]{0,1:T(8,128)(2,1)S(1)}, u32[]{:S(2)}, u32[]{:S(2)}) collective-permute-start(bf16[256,1024]{0,1:T(8,128)(2,1)S(1)} %copy.20), channel_id=1, source_target_pairs={{0,3},{1,4},{2,5},{3,6},{4,7},{5,8},{6,9},{7,10},{8,11},{9,12},{10... | collective-permute-start | bytes 1572872 | tf_op jit(solution)/shard_map/ppermute | solution.py:18
  7.2 129.6 %collective-permute-start.4 = (bf16[256,1024]{0,1:T(8,128)(2,1)S(1)}, bf16[256,1024]{0,1:T(8,128)(2,1)S(1)}, u32[]{:S(2)}, u32[]{:S(2)}) collective-permute-start(bf16[256,1024]{0,1:T(8,128)(2,1)S(1)} %copy.20), channel_id=1, source_target_pairs={{0,2},{1,3},{2,4},{3,5},{4,6},{5,7},{6,8},{7,9},{8,10},{9,11},{10,... | collective-permute-start | bytes 1572872 | tf_op jit(solution)/shard_map/ppermute | solution.py:18
  134.9 16.2 %collective-permute-start.5 = (bf16[256,1024]{0,1:T(8,128)(2,1)S(1)}, bf16[256,1024]{0,1:T(8,128)(2,1)S(1)}, u32[]{:S(2)}, u32[]{:S(2)}) collective-permute-start(bf16[256,1024]{0,1:T(8,128)(2,1)S(1)} %copy.20), channel_id=1, source_target_pairs={{0,1},{1,2},{2,3},{3,4},{4,5},{5,6},{6,7},{7,8},{8,9},{9,10},{10,1... | collective-permute-start | bytes 1572872 | tf_op jit(solution)/shard_map/ppermute | solution.py:18
  136.8 21.0 %collective-permute-start = (bf16[256,1024]{1,0:T(8,128)(2,1)}, bf16[256,1024]{1,0:T(8,128)(2,1)S(1)}, u32[]{:S(2)}, u32[]{:S(2)}) collective-permute-start(bf16[256,1024]{1,0:T(8,128)(2,1)} %param.12), channel_id=1, source_target_pairs={{0,3},{1,4},{2,5},{3,6},{4,7},{5,8},{6,9},{7,10},{8,11},{9,12},{10... | collective-permute-start | bytes 1572872 | tf_op jit(solution)/shard_map/ppermute | solution.py:18
  151.1 24.1 %collective-permute-start.1 = (bf16[256,1024]{1,0:T(8,128)(2,1)S(1)}, bf16[256,1024]{1,0:T(8,128)(2,1)S(1)}, u32[]{:S(2)}, u32[]{:S(2)}) collective-permute-start(bf16[256,1024]{1,0:T(8,128)(2,1)S(1)} %copy-done.2), channel_id=1, source_target_pairs={{0,2},{1,3},{2,4},{3,5},{4,6},{5,7},{6,8},{7,9},{8,10},{9,11},{10,... | collective-permute-start | bytes 1572872 | tf_op jit(solution)/shard_map/ppermute | solution.py:18
  157.9 21.7 %collective-permute-start.2 = (bf16[256,1024]{1,0:T(8,128)(2,1)S(1)}, bf16[256,1024]{1,0:T(8,128)(2,1)S(1)}, u32[]{:S(2)}, u32[]{:S(2)}) collective-permute-start(bf16[256,1024]{1,0:T(8,128)(2,1)S(1)} %copy-done.2), channel_id=1, source_target_pairs={{0,1},{1,2},{2,3},{3,4},{4,5},{5,6},{6,7},{7,8},{8,9},{9,10},{10,1... | collective-permute-start | bytes 1572872 | tf_op jit(solution)/shard_map/ppermute | solution.py:18
  181.1 58.2 %collective-permute-start.9 = (bf16[448,4096]{1,0:T(8,128)(2,1)}, bf16[448,4096]{1,0:T(8,128)(2,1)}, u32[]{:S(2)}, u32[]{:S(2)}) collective-permute-start(bf16[448,4096]{1,0:T(8,128)(2,1)} %collective-permute-done.6), channel_id=1, source_target_pairs={{0,31},{1,0},{2,1},{3,2},{4,3},{5,4},{6,5},{7,6},{8,7},{9,8},{10,9... | collective-permute-start | bytes 11010056 | tf_op jit(solution)/shard_map/ppermute | solution.py:24
  181.1 83.6 %collective-permute-start.10 = (bf16[448,4096]{1,0:T(8,128)(2,1)}, bf16[448,4096]{1,0:T(8,128)(2,1)}, u32[]{:S(2)}, u32[]{:S(2)}) collective-permute-start(bf16[448,4096]{1,0:T(8,128)(2,1)} %collective-permute-done.7), channel_id=1, source_target_pairs={{0,31},{1,0},{2,1},{3,2},{4,3},{5,4},{6,5},{7,6},{8,7},{9,8},{10,9... | collective-permute-start | bytes 11010056 | tf_op jit(solution)/shard_map/ppermute | solution.py:24
  181.2 122.8 %collective-permute-start.11 = (bf16[448,4096]{1,0:T(8,128)(2,1)}, bf16[448,4096]{1,0:T(8,128)(2,1)}, u32[]{:S(2)}, u32[]{:S(2)}) collective-permute-start(bf16[448,4096]{1,0:T(8,128)(2,1)} %collective-permute-done.8), channel_id=1, source_target_pairs={{0,31},{1,0},{2,1},{3,2},{4,3},{5,4},{6,5},{7,6},{8,7},{9,8},{10,9... | collective-permute-start | bytes 11010056 | tf_op jit(solution)/shard_map/ppermute | solution.py:24
  231.6 5.4 %copy-start = (bf16[256,4096]{0,1:T(8,128)(2,1)}, bf16[256,4096]{0,1:T(8,128)(2,1)S(1)}, u32[]{:S(2)}) copy-start(bf16[256,4096]{0,1:T(8,128)(2,1)S(1)} %get-tuple-element.188) | copy-start | bytes 6291460
  231.6 5.4 %copy-start.3 = (f32[4096]{0:T(1024)S(1)}, f32[4096]{0:T(1024)}, u32[]{:S(2)}) copy-start(f32[4096]{0:T(1024)} %param.16) | copy-start | bytes 49156
  234.5 2.5 copy-start.1
  237.0 2.7 copy-start.5
  239.3 104.1 %collective-permute-start.12 = (bf16[448,4096]{1,0:T(8,128)(2,1)}, bf16[448,4096]{1,0:T(8,128)(2,1)}, u32[]{:S(2)}, u32[]{:S(2)}) collective-permute-start(bf16[448,4096]{1,0:T(8,128)(2,1)} %collective-permute-done.9), channel_id=1, source_target_pairs={{0,31},{1,0},{2,1},{3,2},{4,3},{5,4},{6,5},{7,6},{8,7},{9,8},{10,9... | collective-permute-start | bytes 11010056 | tf_op jit(solution)/shard_map/ppermute | solution.py:24
  264.7 118.0 %collective-permute-start.13 = (bf16[448,4096]{1,0:T(8,128)(2,1)}, bf16[448,4096]{1,0:T(8,128)(2,1)}, u32[]{:S(2)}, u32[]{:S(2)}) collective-permute-start(bf16[448,4096]{1,0:T(8,128)(2,1)} %collective-permute-done.10), channel_id=1, source_target_pairs={{0,31},{1,0},{2,1},{3,2},{4,3},{5,4},{6,5},{7,6},{8,7},{9,8},{10,9... | collective-permute-start | bytes 11010056 | tf_op jit(solution)/shard_map/ppermute | solution.py:24
  304.0 118.0 %collective-permute-start.14 = (bf16[448,4096]{1,0:T(8,128)(2,1)}, bf16[448,4096]{1,0:T(8,128)(2,1)}, u32[]{:S(2)}, u32[]{:S(2)}) collective-permute-start(bf16[448,4096]{1,0:T(8,128)(2,1)} %collective-permute-done.11), channel_id=1, source_target_pairs={{0,31},{1,0},{2,1},{3,2},{4,3},{5,4},{6,5},{7,6},{8,7},{9,8},{10,9... | collective-permute-start | bytes 11010056 | tf_op jit(solution)/shard_map/ppermute | solution.py:24
where the time goes:
time: 433 us; the launch traced here: 432 us
  waiting for transfers between devices  269 us (62%)
  matrix products  82.3 us (19%)
  starting transfers between devices  44.1 us (10%)
  local copies, waits for them, and re-layouts  17.7 us (4%)
  other arithmetic  17.2 us (4%)
    ppermute x9, waiting for transfers between devices, shifted(): return lax.ppermute(value, axis, pairs)  141 us
    ppermute x6, waiting for transfers between devices, passed_along(): return lax.ppermute(value, axis, pairs)  128 us
    ppermute x6, starting transfers between devices, passed_along(): return lax.ppermute(value, axis, pairs)  42.5 us
    dot_general x4, matrix products, shard_term(): return jnp.dot(hidden, down_rows, preferred_element_type=jnp.float32)  40.3 us
    dot_general x8, matrix products, group_of_head(): jnp.einsum('rtk,kd->rtd', weights.astype(jnp.bfloat16), value_block, pref...  17.3 us
    dot_general x8, matrix products, group_of_head(): jnp.einsum('trd,kd->rtk', query_block, key_block, preferred_element_type=...  13.9 us
    dot_general x4, matrix products, shard_term(): lax.dot_general(rows_in, gate_rows, contract, preferred_element_type=jnp....  10.8 us
    dynamic_slice x16, local copies, waits for them, and re-layouts, group_of_head(): lax.dynamic_slice_in_dim(query_states, group_index * heads_per_group * HE...  8.85 us
  transfers between devices with their start and end apart: 15, of which 7 were waited for; matrix products, arithmetic and copies ran while one was open for 25% of the time, Pallas kernels for 0%

commit v1 on v0

--- a/solution.py
+++ b/solution.py
@@ -104,15 +104,14 @@
     normed = (
         stream * lax.rsqrt(jnp.mean(stream * stream, axis=-1, keepdims=True) + 1e-05) * norm_gain
     ).astype(jnp.bfloat16)
-    ffn_total = shard_term(normed, gate_weight, up_weight, down_weight)
-    current_weights = (gate_weight, up_weight, down_weight)
+    met = [normed] + [shifted(normed, "blk", offset) for offset in range(1, FFN_STEPS)]
+    ffn_total = shard_term(met[0], gate_weight, up_weight, down_weight)
+    parts = []
     for offset in range(1, FFN_STEPS):
-        current_weights = shifted(
-            (current_weights[0], current_weights[1], current_weights[2]), "blk", -1
-        )
-        ffn_total = ffn_total + shard_term(
-            normed, current_weights[0], current_weights[1], current_weights[2]
-        )
+        part = shard_term(met[offset], gate_weight, up_weight, down_weight).astype(jnp.bfloat16)
+        parts.append(shifted(part, "blk", -offset))
+    for part in parts:
+        ffn_total = ffn_total + part.astype(jnp.float32)
     return (attended, ffn_total.astype(jnp.bfloat16))
 
 

time: 433 us -> 391 us (0.903)
  the two profiles are of different devices: /device:TPU:19 before, /device:TPU:30 now
where the time goes in v1:
time: 391 us; the launch traced here: 388 us
  waiting for transfers between devices  161 us (41%)
  starting transfers between devices  106 us (27%)
  matrix products  82.8 us (21%)
  local copies, waits for them, and re-layouts  18.8 us (5%)
  other arithmetic  17.9 us (5%)
    ppermute x6, waiting for transfers between devices, shifted(): return lax.ppermute(value, axis, pairs)  131 us
    ppermute x6, starting transfers between devices, shifted(): return lax.ppermute(value, axis, pairs)  92.9 us
    dot_general x4, matrix products, shard_term(): return jnp.dot(hidden, down_rows, preferred_element_type=jnp.float32)  39 us
    ppermute x6, waiting for transfers between devices, passed_along(): return lax.ppermute(value, axis, pairs)  29.7 us
    dot_general x8, matrix products, group_of_head(): jnp.einsum('rtk,kd->rtd', weights.astype(jnp.bfloat16), value_block, pref...  17.3 us
    dot_general x8, matrix products, group_of_head(): jnp.einsum('trd,kd->rtk', query_block, key_block, preferred_element_type=...  13.9 us
    ppermute x6, starting transfers between devices, passed_along(): return lax.ppermute(value, axis, pairs)  13.3 us
    dot_general x4, matrix products, shard_term(): lax.dot_general(rows_in, gate_rows, contract, preferred_element_type=jnp....  12.6 us
  transfers between devices with their start and end apart: 12, of which 8 were waited for; matrix products, arithmetic and copies ran while one was open for 13% of the time, Pallas kernels for 0%

profile of v1, /device:TPU:30, one launch (start us, length us, event | category | flops | bytes accessed | tf_op | source)
XLA Modules:
  0.0 388.0 jit_solution(9735890822431839255)
XLA Ops:
  4.6 1.9 collective-permute-start.5
  9.1 4.1 %copy.25 = bf16[256,4096]{0,1:T(8,128)(2,1)} copy(bf16[256,4096]{1,0:T(8,128)(2,1)} %param.15) | data formatting | bytes 4194304 | tf_op args[4]
  13.2 6.2 %collective-permute-start.2 = (bf16[256,1024]{1,0:T(8,128)(2,1)S(1)}, bf16[256,1024]{1,0:T(8,128)(2,1)S(1)}, u32[]{:S(2)}, u32[]{:S(2)}) collective-permute-start(bf16[256,1024]{1,0:T(8,128)(2,1)S(1)} %copy-done.1), channel_id=1, source_target_pairs={{0,1},{1,2},{2,3},{3,4},{4,5},{5,6},{6,7},{7,8},{8,9},{9,10},{10,1... | collective-permute-start | bytes 1572872 | tf_op jit(solution)/shard_map/ppermute | solution.py:18
  19.5 9.2 %collective-permute-done.4 = bf16[256,1024]{0,1:T(8,128)(2,1)S(1)} collective-permute-done((bf16[256,1024]{0,1:T(8,128)(2,1)S(1)}, bf16[256,1024]{0,1:T(8,128)(2,1)S(1)}, u32[]{:S(2)}, u32[]{:S(2)}) %collective-permute-start.4) | collective-permute-done | bytes 524320 | tf_op jit(solution)/shard_map/ppermute | solution.py:18
  30.1 2.7 pad_maximum_fusion.1
  32.8 18.3 %collective-permute-done.1 = bf16[256,1024]{1,0:T(8,128)(2,1)S(1)} collective-permute-done((bf16[256,1024]{1,0:T(8,128)(2,1)}, bf16[256,1024]{1,0:T(8,128)(2,1)S(1)}, u32[]{:S(2)}, u32[]{:S(2)}) %collective-permute-start.1) | collective-permute-done | bytes 524320 | tf_op jit(solution)/shard_map/ppermute | solution.py:18
  53.4 50.2 %while.16 = (s32[]{:T(128)}, bf16[256,4096]{0,1:T(8,128)(2,1)S(1)}, bf16[1024,1024]{1,0:T(8,128)(2,1)}, bf16[256,4096]{1,0:T(8,128)(2,1)}, bf16[1024,1024]{0,1:T...) while((s32[]{:T(128)}, bf16[256,4096]{0,1:T(8,128)(2,1)S(1)}, ...), condition=%wide.region_3.4_spmd.clone, body=%wide.region_0.3_spmd.clone.sunk | while | flops 549451776 | bytes 16279793 | solution.py:97
  57.5 2.2 fusion.84
  63.8 2.2 fusion.84
  70.0 2.2 fusion.84
  76.3 2.2 fusion.84
  82.6 2.2 fusion.84
  88.9 2.2 fusion.84
  95.1 2.2 fusion.84
  101.4 2.2 fusion.84
  103.6 2.5 multiply_reduce_fusion
  106.2 1.8 multiply_convert_fusion
  108.0 7.3 %collective-permute-start.8 = (bf16[256,4096]{0,1:T(8,128)(2,1)}, bf16[256,4096]{0,1:T(8,128)(2,1)}, u32[]{:S(2)}, u32[]{:S(2)}) collective-permute-start(bf16[256,4096]{0,1:T(8,128)(2,1)} %multiply_convert_fusion), channel_id=1, source_target_pairs={{0,2},{1,3},{2,4},{3,5},{4,6},{5,7},{6,8},{7,9},{8,10},{9,11},{10,... | collective-permute-start | bytes 6291464 | tf_op jit(solution)/shard_map/ppermute | solution.py:24
  115.3 6.6 %collective-permute-start.10 = (bf16[256,4096]{0,1:T(8,128)(2,1)}, bf16[256,4096]{0,1:T(8,128)(2,1)}, u32[]{:S(2)}, u32[]{:S(2)}) collective-permute-start(bf16[256,4096]{0,1:T(8,128)(2,1)} %multiply_convert_fusion), channel_id=1, source_target_pairs={{0,3},{1,4},{2,5},{3,6},{4,7},{5,8},{6,9},{7,10},{8,11},{9,12},{10... | collective-permute-start | bytes 6291464 | tf_op jit(solution)/shard_map/ppermute | solution.py:24
  122.0 28.0 %collective-permute-done.6 = bf16[256,4096]{0,1:T(8,128)(2,1)S(1)} collective-permute-done((bf16[256,4096]{0,1:T(8,128)(2,1)}, bf16[256,4096]{0,1:T(8,128)(2,1)S(1)}, u32[]{:S(2)}, u32[]{:S(2)}) %collective-permute-start.6) | collective-permute-done | bytes 2097184 | tf_op jit(solution)/shard_map/ppermute | solution.py:24
  152.4 9.3 %convolution_convert_fusion.2 = bf16[256,4096]{1,0:T(8,128)(2,1)} fusion(bf16[448,4096]{1,0:T(8,128)(2,1)} %param.19, f32[256,448]{0,1:T(8,128)S(1)} %fusion.49, bf16[448,4096]{1,0:T(8,128)(2,1)} %param.18, bf16[256,4096]{0,1:T(8,128)(2,1)} %copy-done.5), kind=kOutput, calls=%fused_computation.25 | convolution fusion | flops 1880784896 | bytes 11993088 | tf_op jit(solution)/shard_map/dot_general | solution.py:32
  161.7 22.2 %collective-permute-done.8 = bf16[256,4096]{0,1:T(8,128)(2,1)} collective-permute-done((bf16[256,4096]{0,1:T(8,128)(2,1)}, bf16[256,4096]{0,1:T(8,128)(2,1)}, u32[]{:S(2)}, u32[]{:S(2)}) %collective-permute-start.8) | collective-permute-done | bytes 2097184 | tf_op jit(solution)/shard_map/ppermute | solution.py:24
  184.0 3.8 fusion.50
  187.8 9.3 %convolution_convert_fusion.1 = bf16[256,4096]{1,0:T(8,128)(2,1)} fusion(bf16[448,4096]{1,0:T(8,128)(2,1)} %param.19, f32[256,448]{0,1:T(8,128)S(1)} %fusion.50, bf16[448,4096]{1,0:T(8,128)(2,1)} %param.18, bf16[256,4096]{0,1:T(8,128)(2,1)} %collective-permute-done.8), kind=kOutput, calls=%fused_computation.24 | convolution fusion | flops 1880784896 | bytes 11993088 | tf_op jit(solution)/shard_map/dot_general | solution.py:32
  197.1 31.8 %collective-permute-done.10 = bf16[256,4096]{0,1:T(8,128)(2,1)} collective-permute-done((bf16[256,4096]{0,1:T(8,128)(2,1)}, bf16[256,4096]{0,1:T(8,128)(2,1)}, u32[]{:S(2)}, u32[]{:S(2)}) %collective-permute-start.10) | collective-permute-done | bytes 2097184 | tf_op jit(solution)/shard_map/ppermute | solution.py:24
  228.9 3.8 fusion.51
  232.7 9.3 %convolution_convert_fusion = bf16[256,4096]{1,0:T(8,128)(2,1)} fusion(bf16[448,4096]{1,0:T(8,128)(2,1)} %param.19, f32[256,448]{0,1:T(8,128)S(1)} %fusion.51, bf16[448,4096]{1,0:T(8,128)(2,1)} %param.18, bf16[256,4096]{0,1:T(8,128)(2,1)} %collective-permute-done.10), kind=kOutput, calls=%fused_computation.23 | convolution fusion | flops 1880784896 | bytes 11993088 | tf_op jit(solution)/shard_map/dot_general | solution.py:32
  242.0 78.9 %collective-permute-start.11 = (bf16[256,4096]{1,0:T(8,128)(2,1)}, bf16[256,4096]{1,0:T(8,128)(2,1)}, u32[]{:S(2)}, u32[]{:S(2)}) collective-permute-start(bf16[256,4096]{1,0:T(8,128)(2,1)} %convolution_convert_fusion), channel_id=1, source_target_pairs={{0,29},{1,30},{2,31},{3,0},{4,1},{5,2},{6,3},{7,4},{8,5},{9,6},{10... | collective-permute-start | bytes 6291464 | tf_op jit(solution)/shard_map/ppermute | solution.py:24
  320.9 2.8 copy.26
  323.8 3.8 fusion.48
  327.6 49.3 %collective-permute-done.11 = bf16[256,4096]{1,0:T(8,128)(2,1)} collective-permute-done((bf16[256,4096]{1,0:T(8,128)(2,1)}, bf16[256,4096]{1,0:T(8,128)(2,1)}, u32[]{:S(2)}, u32[]{:S(2)}) %collective-permute-start.11) | collective-permute-done | bytes 2097184 | tf_op jit(solution)/shard_map/ppermute | solution.py:24
  376.9 11.1 %add_convert_fusion = bf16[256,4096]{1,0:T(8,128)(2,1)} fusion(bf16[256,4096]{1,0:T(8,128)(2,1)} %collective-permute-done.11, bf16[256,4096]{1,0:T(8,128)(2,1)} %collective-permute-done.9, bf16[256,4096]{1,0:T(8,128)(2,1)} %collective-permute-done.7, bf16[448,4096]{1,0:T(8,128)(2,1)} %param.19, bf16[448,4096]{1,0:T(8,128)(2,1)} %param.18, ...), kind=kOutput, calls=%fused_computation.26 | convolution fusion | flops 1887076352 | bytes 18284544 | tf_op jit(solution)/shard_map/dot_general | solution.py:32
  (80 shorter events, 45.1 us)
Async XLA Ops:
  0.6 12.6 %copy-start.1 = (bf16[256,1024]{1,0:T(8,128)(2,1)S(1)}, bf16[256,1024]{1,0:T(8,128)(2,1)}, u32[]{:S(2)}) copy-start(bf16[256,1024]{1,0:T(8,128)(2,1)} %param.12) | copy-start | bytes 1572868
  0.6 18.8 %copy-start.3 = (s32[256]{0:T(256)S(1)}, s32[256]{0:T(256)}, u32[]{:S(2)}) copy-start(s32[256]{0:T(256)} %param.14) | copy-start | bytes 3076
  2.0 11.2 %collective-permute-start.3 = (bf16[256,1024]{0,1:T(8,128)(2,1)S(1)}, bf16[256,1024]{0,1:T(8,128)(2,1)S(1)}, u32[]{:S(2)}, u32[]{:S(2)}) collective-permute-start(bf16[256,1024]{0,1:T(8,128)(2,1)S(1)} %copy.20), channel_id=1, source_target_pairs={{0,3},{1,4},{2,5},{3,6},{4,7},{5,8},{6,9},{7,10},{8,11},{9,12},{10... | collective-permute-start | bytes 1572872 | tf_op jit(solution)/shard_map/ppermute | solution.py:18
  3.3 25.4 %collective-permute-start.4 = (bf16[256,1024]{0,1:T(8,128)(2,1)S(1)}, bf16[256,1024]{0,1:T(8,128)(2,1)S(1)}, u32[]{:S(2)}, u32[]{:S(2)}) collective-permute-start(bf16[256,1024]{0,1:T(8,128)(2,1)S(1)} %copy.20), channel_id=1, source_target_pairs={{0,2},{1,3},{2,4},{3,5},{4,6},{5,7},{6,8},{7,9},{8,10},{9,11},{10,... | collective-permute-start | bytes 1572872 | tf_op jit(solution)/shard_map/ppermute | solution.py:18
  4.6 25.6 %collective-permute-start.5 = (bf16[256,1024]{0,1:T(8,128)(2,1)S(1)}, bf16[256,1024]{0,1:T(8,128)(2,1)}, u32[]{:S(2)}, u32[]{:S(2)}) collective-permute-start(bf16[256,1024]{0,1:T(8,128)(2,1)S(1)} %copy.20), channel_id=1, source_target_pairs={{0,1},{1,2},{2,3},{3,4},{4,5},{5,6},{6,7},{7,8},{8,9},{9,10},{10,1... | collective-permute-start | bytes 1572872 | tf_op jit(solution)/shard_map/ppermute | solution.py:18
  6.5 26.3 %collective-permute-start = (bf16[256,1024]{1,0:T(8,128)(2,1)}, bf16[256,1024]{1,0:T(8,128)(2,1)S(1)}, u32[]{:S(2)}, u32[]{:S(2)}) collective-permute-start(bf16[256,1024]{1,0:T(8,128)(2,1)} %param.12), channel_id=1, source_target_pairs={{0,3},{1,4},{2,5},{3,6},{4,7},{5,8},{6,9},{7,10},{8,11},{9,12},{10... | collective-permute-start | bytes 1572872 | tf_op jit(solution)/shard_map/ppermute | solution.py:18
  7.8 43.3 %collective-permute-start.1 = (bf16[256,1024]{1,0:T(8,128)(2,1)}, bf16[256,1024]{1,0:T(8,128)(2,1)S(1)}, u32[]{:S(2)}, u32[]{:S(2)}) collective-permute-start(bf16[256,1024]{1,0:T(8,128)(2,1)} %param.12), channel_id=1, source_target_pairs={{0,2},{1,3},{2,4},{3,5},{4,6},{5,7},{6,8},{7,9},{8,10},{9,11},{10,... | collective-permute-start | bytes 1572872 | tf_op jit(solution)/shard_map/ppermute | solution.py:18
  13.2 38.6 %collective-permute-start.2 = (bf16[256,1024]{1,0:T(8,128)(2,1)S(1)}, bf16[256,1024]{1,0:T(8,128)(2,1)S(1)}, u32[]{:S(2)}, u32[]{:S(2)}) collective-permute-start(bf16[256,1024]{1,0:T(8,128)(2,1)S(1)} %copy-done.1), channel_id=1, source_target_pairs={{0,1},{1,2},{2,3},{3,4},{4,5},{5,6},{6,7},{7,8},{8,9},{9,10},{10,1... | collective-permute-start | bytes 1572872 | tf_op jit(solution)/shard_map/ppermute | solution.py:18
  103.6 2.5 copy-start
  103.6 2.5 copy-start.2
  106.1 45.2 %copy-start.4 = (bf16[448,4096]{1,0:T(8,128)(2,1)S(1)}, bf16[448,4096]{1,0:T(8,128)(2,1)}, u32[]{:S(2)}) copy-start(bf16[448,4096]{1,0:T(8,128)(2,1)} %param.17) | copy-start | bytes 11010052
  108.0 42.0 %collective-permute-start.6 = (bf16[256,4096]{0,1:T(8,128)(2,1)}, bf16[256,4096]{0,1:T(8,128)(2,1)S(1)}, u32[]{:S(2)}, u32[]{:S(2)}) collective-permute-start(bf16[256,4096]{0,1:T(8,128)(2,1)} %multiply_convert_fusion), channel_id=1, source_target_pairs={{0,1},{1,2},{2,3},{3,4},{4,5},{5,6},{6,7},{7,8},{8,9},{9,10},{10,1... | collective-permute-start | bytes 6291464 | tf_op jit(solution)/shard_map/ppermute | solution.py:24
  108.0 75.9 %collective-permute-start.8 = (bf16[256,4096]{0,1:T(8,128)(2,1)}, bf16[256,4096]{0,1:T(8,128)(2,1)}, u32[]{:S(2)}, u32[]{:S(2)}) collective-permute-start(bf16[256,4096]{0,1:T(8,128)(2,1)} %multiply_convert_fusion), channel_id=1, source_target_pairs={{0,2},{1,3},{2,4},{3,5},{4,6},{5,7},{6,8},{7,9},{8,10},{9,11},{10,... | collective-permute-start | bytes 6291464 | tf_op jit(solution)/shard_map/ppermute | solution.py:24
  115.3 113.6 %collective-permute-start.10 = (bf16[256,4096]{0,1:T(8,128)(2,1)}, bf16[256,4096]{0,1:T(8,128)(2,1)}, u32[]{:S(2)}, u32[]{:S(2)}) collective-permute-start(bf16[256,4096]{0,1:T(8,128)(2,1)} %multiply_convert_fusion), channel_id=1, source_target_pairs={{0,3},{1,4},{2,5},{3,6},{4,7},{5,8},{6,9},{7,10},{8,11},{9,12},{10... | collective-permute-start | bytes 6291464 | tf_op jit(solution)/shard_map/ppermute | solution.py:24
  150.0 1.3 copy-start.5
  161.7 165.9 %collective-permute-start.7 = (bf16[256,4096]{1,0:T(8,128)(2,1)}, bf16[256,4096]{1,0:T(8,128)(2,1)}, u32[]{:S(2)}, u32[]{:S(2)}) collective-permute-start(bf16[256,4096]{1,0:T(8,128)(2,1)} %convolution_convert_fusion.2), channel_id=1, source_target_pairs={{0,31},{1,0},{2,1},{3,2},{4,3},{5,4},{6,5},{7,6},{8,7},{9,8},{10,9... | collective-permute-start | bytes 6291464 | tf_op jit(solution)/shard_map/ppermute | solution.py:24
  197.1 130.5 %collective-permute-start.9 = (bf16[256,4096]{1,0:T(8,128)(2,1)}, bf16[256,4096]{1,0:T(8,128)(2,1)}, u32[]{:S(2)}, u32[]{:S(2)}) collective-permute-start(bf16[256,4096]{1,0:T(8,128)(2,1)} %convolution_convert_fusion.1), channel_id=1, source_target_pairs={{0,30},{1,31},{2,0},{3,1},{4,2},{5,3},{6,4},{7,5},{8,6},{9,7},{10,... | collective-permute-start | bytes 6291464 | tf_op jit(solution)/shard_map/ppermute | solution.py:24
  242.0 134.9 %collective-permute-start.11 = (bf16[256,4096]{1,0:T(8,128)(2,1)}, bf16[256,4096]{1,0:T(8,128)(2,1)}, u32[]{:S(2)}, u32[]{:S(2)}) collective-permute-start(bf16[256,4096]{1,0:T(8,128)(2,1)} %convolution_convert_fusion), channel_id=1, source_target_pairs={{0,29},{1,30},{2,31},{3,0},{4,1},{5,2},{6,3},{7,4},{8,5},{9,6},{10... | collective-permute-start | bytes 6291464 | tf_op jit(solution)/shard_map/ppermute | solution.py:24

commit v2 on v1

v2 whole, which is shorter than its diff:
```python
import functools
import math

import jax
import jax.numpy as jnp
from jax import lax
from jax.experimental import pallas as pl
from jax.experimental.pallas import tpu as pltpu
from jax.sharding import PartitionSpec as P

HEAD_SIZE = 128
KEY_VALUE_HEADS = 8
HEADS_PER_GROUP = 4
WINDOW_BLOCKS = 4
FFN_STEPS = 4
CHUNK = HEADS_PER_GROUP * HEAD_SIZE
PAIR = 2 * HEAD_SIZE
MESH = pl.DeviceIdType.MESH
NT = (((1,), (1,)), ((), ()))


def layer_kernel(
    count,
    q_hbm,
    k_hbm,
    v_hbm,
    pos_ref,
    res_hbm,
    gain_ref,
    gate_hbm,
    up_hbm,
    down_hbm,
    attended_hbm,
    ffn_hbm,
    q,
    k_own,
    v_own,
    res,
    gate,
    up,
    down,
    k_in,
    v_in,
    bias,
    s_own,
    s_in,
    square,
    rs_own,
    rs_in,
    acc_gate,
    acc_up,
    hidden,
    part,
    x_in,
    r_in,
    att,
    ffn,
    load_sem,
    att_sem,
    ffn_sem,
    kv_send,
    kv_recv,
    s_send,
    s_recv,
    rs_send,
    rs_recv,
    p_send,
    p_recv,
):
    rows, width = q.shape
    groups = KEY_VALUE_HEADS
    pairs = groups // 2
    me = lax.axis_index("blk")
    core = lax.rem(me, 2)

    def at(offset):
        return lax.rem(me + offset + count, count)

    two_on = at(2)
    third, third_slot = at(1 + 2 * core), 2 * core
    sibling, sibling_slot = at(1 - 2 * core), 2 - 2 * core
    routes = ((two_on, 1), (third, third_slot), (sibling, sibling_slot))

    loads = [
        pltpu.make_async_copy(src, dst, load_sem.at[i])
        for i, (src, dst) in enumerate(
            (
                (k_hbm, k_own),
                (v_hbm, v_own),
                (q_hbm, q),
                (res_hbm, res),
                (gate_hbm, gate),
                (up_hbm, up),
                (down_hbm, down),
            )
        )
    ]
    for load in loads:
        load.start()

    barrier = pltpu.get_barrier_semaphore()
    for offset in (1, 2, 3, -1, -2, -3):
        pl.semaphore_signal(barrier, inc=1, device_id=(at(offset),), device_id_type=MESH)
    pl.semaphore_wait(barrier, 6)

    def kv_copy(which, route, j):
        device, slot = routes[route]
        own, arrived = ((k_hbm, k_in), (v_hbm, v_in))[which]
        if route == 2:
            src = arrived.at[1, j]
        else:
            src = own.at[:, pl.ds(pl.multiple_of(j * PAIR, PAIR), PAIR)]
        return pltpu.make_async_remote_copy(
            src_ref=src,
            dst_ref=arrived.at[slot, j],
            send_sem=kv_send.at[which, route, j],
            recv_sem=kv_recv.at[which, slot, j],
            device_id=(device,),
            device_id_type=MESH,
        )

    def kv_arrival(which, slot, j):
        arrived = (k_in, v_in)[which]
        pltpu.make_async_copy(arrived.at[slot, j], arrived.at[slot, j], kv_recv.at[which, slot, j]).wait()

    def s_copy(route, g):
        device, slot = routes[route]
        return pltpu.make_async_remote_copy(
            src_ref=s_in.at[1, g] if route == 2 else s_own.at[g],
            dst_ref=s_in.at[slot, g],
            send_sem=s_send.at[route, g],
            recv_sem=s_recv.at[slot, g],
            device_id=(device,),
            device_id_type=MESH,
        )

    def s_arrival(slot, g):
        pltpu.make_async_copy(s_in.at[slot, g], s_in.at[slot, g], s_recv.at[slot, g]).wait()

    def rs_copy(route):
        device, slot = routes[route]
        return pltpu.make_async_remote_copy(
            src_ref=rs_in.at[1] if route == 2 else rs_own,
            dst_ref=rs_in.at[slot],
            send_sem=rs_send.at[route],
            recv_sem=rs_recv.at[slot],
            device_id=(device,),
            device_id_type=MESH,
        )

    def rs_arrival(slot):
        pltpu.make_async_copy(rs_in.at[slot], rs_in.at[slot], rs_recv.at[slot]).wait()

    def p_copy(kind, g):
        device = (sibling, at(-2), at(2 * core - 3))[kind]
        dst = x_in.at[g] if kind == 0 else r_in.at[kind - 1, g]
        return pltpu.make_async_remote_copy(
            src_ref=part.at[kind, g],
            dst_ref=dst,
            send_sem=p_send.at[kind, g],
            recv_sem=p_recv.at[kind, g],
            device_id=(device,),
            device_id_type=MESH,
        )

    def p_arrival(kind, g):
        dst = x_in.at[g] if kind == 0 else r_in.at[kind - 1, g]
        pltpu.make_async_copy(dst, dst, p_recv.at[kind, g]).wait()

    def each(limit):
        def run(body):
            lax.fori_loop(0, limit, lambda i, c: (body(i), c)[1], 0)

        return run

    @each(pairs)
    def _(j):
        for which in range(2):
            for route in range(2):
                kv_copy(which, route, j).start()

    row = lax.broadcasted_iota(jnp.int32, (rows, rows), 0)
    column = lax.broadcasted_iota(jnp.int32, (rows, rows), 1)
    for d in range(WINDOW_BLOCKS):
        key = column - d * rows
        seen = (key <= row) & (key >= row - pos_ref[...])
        bias[d] = jnp.where(seen, 0.0, -jnp.inf)
    square[...] = jnp.zeros_like(square)
    for load in loads[:4]:
        load.wait()

    factor = math.log2(math.e) / math.sqrt(HEAD_SIZE)

    @each(pairs)
    def _(j):
        for which in range(2):
            kv_arrival(which, 1, j)
            kv_copy(which, 2, j).start()
        for which in range(2):
            kv_arrival(which, 0, j)
            kv_arrival(which, 2, j)
        for half in range(2):
            g = 2 * j + half
            here = pl.ds(half * HEAD_SIZE, HEAD_SIZE)
            kv_cols = pl.ds(pl.multiple_of(g * HEAD_SIZE, HEAD_SIZE), HEAD_SIZE)
            keys = [k_own[:, kv_cols]] + [k_in[s, j, :, here] for s in range(3)]
            values = [v_own[:, kv_cols]] + [v_in[s, j, :, here] for s in range(3)]
            for h in range(HEADS_PER_GROUP):
                cols = pl.ds(pl.multiple_of(g * CHUNK + h * HEAD_SIZE, HEAD_SIZE), HEAD_SIZE)
                inner = pl.ds(h * HEAD_SIZE, HEAD_SIZE)
                query = q[:, cols]
                scores = [
                    lax.dot_general(query, keys[d], NT, preferred_element_type=jnp.float32) + bias[d]
                    for d in range(WINDOW_BLOCKS)
                ]
                top = functools.reduce(jnp.maximum, scores)
                top = jnp.max(top, axis=1, keepdims=True)
                weights = [jnp.exp2((score - top) * factor) for score in scores]
                total = jnp.sum(functools.reduce(jnp.add, weights), axis=1, keepdims=True)
                mixed = functools.reduce(
                    jnp.add,
                    [
                        jnp.dot(w.astype(jnp.bfloat16), v, preferred_element_type=jnp.float32)
                        for w, v in zip(weights, values)
                    ],
                )
                attended = (mixed / total).astype(jnp.bfloat16)
                att[:, cols] = attended
                stream = res[:, cols].astype(jnp.float32) + attended.astype(jnp.float32)
                square[...] += stream * stream
                s_own[g, :, inner] = (stream * gain_ref[:, cols]).astype(jnp.bfloat16)
            s_copy(0, g).start()
            s_copy(1, g).start()

    att_copy = pltpu.make_async_copy(att, attended_hbm, att_sem)
    att_copy.start()
    mean = jnp.sum(square[...], axis=1, keepdims=True) * (1.0 / width)
    rs_own[...] = jnp.broadcast_to(lax.rsqrt(mean + 1e-05), rs_own.shape)
    rs_copy(0).start()
    rs_copy(1).start()
    for load in loads[4:]:
        load.wait()
    acc_gate[...] = jnp.zeros_like(acc_gate)
    acc_up[...] = jnp.zeros_like(acc_up)

    def add_chunk(place, chunk, g):
        cols = pl.ds(pl.multiple_of(g * CHUNK, CHUNK), CHUNK)
        acc_gate[place] += lax.dot_general(chunk, gate[:, cols], NT, preferred_element_type=jnp.float32)
        acc_up[place] += lax.dot_general(chunk, up[:, cols], NT, preferred_element_type=jnp.float32)

    def make_hidden(place, scale):
        gate_value = acc_gate[place] * scale[:, :1]
        up_value = acc_up[place] * scale[:, :1]
        silu = gate_value / (1.0 + jnp.exp(-gate_value))
        hidden[place] = (silu * up_value).astype(jnp.bfloat16)

    def down_chunk(place, g):
        cols = pl.ds(pl.multiple_of(g * CHUNK, CHUNK), CHUNK)
        return jnp.dot(hidden[place], down[:, cols], preferred_element_type=jnp.float32)

    @each(groups)
    def _(g):
        s_arrival(1, g)
        s_copy(2, g).start()
        add_chunk(3, s_own[g], g)
        add_chunk(1, s_in[1, g], g)

    rs_arrival(1)
    rs_copy(2).start()
    make_hidden(3, rs_own[...])
    make_hidden(1, rs_in[1])

    @each(groups)
    def _(g):
        s_arrival(2 - 2 * core, g)
        add_chunk(2, s_in[2 - 2 * core, g], g)

    rs_arrival(2 - 2 * core)
    make_hidden(2, rs_in[2 - 2 * core])

    @each(groups)
    def _(g):
        part[2, g] = down_chunk(2, g).astype(jnp.bfloat16)
        p_copy(2, g).start()

    @each(groups)
    def _(g):
        s_arrival(2 * core, g)
        add_chunk(0, s_in[2 * core, g], g)

    rs_arrival(2 * core)
    make_hidden(0, rs_in[2 * core])

    @each(groups)
    def _(g):
        part[0, g] = down_chunk(0, g).astype(jnp.bfloat16)
        p_copy(0, g).start()

    @each(groups)
    def _(g):
        mine = down_chunk(1, g)
        p_arrival(0, g)
        part[1, g] = (mine + x_in[g].astype(jnp.float32)).astype(jnp.bfloat16)
        p_copy(1, g).start()

    @each(groups)
    def _(g):
        cols = pl.ds(pl.multiple_of(g * CHUNK, CHUNK), CHUNK)
        mine = down_chunk(3, g)
        p_arrival(2, g)
        p_arrival(1, g)
        total = mine + r_in[0, g].astype(jnp.float32) + r_in[1, g].astype(jnp.float32)
        ffn[:, cols] = total.astype(jnp.bfloat16)

    ffn_copy = pltpu.make_async_copy(ffn, ffn_hbm, ffn_sem)
    ffn_copy.start()

    @each(pairs)
    def _(j):
        for which in range(2):
            for route in range(3):
                kv_copy(which, route, j).wait_send()

    @each(groups)
    def _(g):
        for route in range(3):
            s_copy(route, g).wait_send()
            p_copy(route, g).wait_send()

    for route in range(3):
        rs_copy(route).wait_send()
    att_copy.wait()
    ffn_copy.wait()


def per_device(count, q, k, v, positions, residual, gain, gate, up, down):
    rows, width = q.shape
    units = gate.shape[0]
    groups = KEY_VALUE_HEADS
    pairs = groups // 2
    bf16, f32 = jnp.bfloat16, jnp.float32
    any_spec = pl.BlockSpec(memory_space=pl.ANY)
    vmem_spec = pl.BlockSpec(memory_space=pltpu.VMEM)
    dma = pltpu.SemaphoreType.DMA
    return pl.pallas_call(
        functools.partial(layer_kernel, count),
        out_shape=(jax.ShapeDtypeStruct((rows, width), bf16),) * 2,
        in_specs=[any_spec, any_spec, any_spec, vmem_spec, any_spec, vmem_spec] + [any_spec] * 3,
        out_specs=(any_spec, any_spec),
        scratch_shapes=[
            pltpu.VMEM((rows, width), bf16),
            pltpu.VMEM(k.shape, bf16),
            pltpu.VMEM(v.shape, bf16),
            pltpu.VMEM((rows, width), bf16),
            pltpu.VMEM((units, width), bf16),
            pltpu.VMEM((units, width), bf16),
            pltpu.VMEM((units, width), bf16),
            pltpu.VMEM((3, pairs, rows, PAIR), bf16),
            pltpu.VMEM((3, pairs, rows, PAIR), bf16),
            pltpu.VMEM((WINDOW_BLOCKS, rows, rows), f32),
            pltpu.VMEM((groups, rows, CHUNK), bf16),
            pltpu.VMEM((3, groups, rows, CHUNK), bf16),
            pltpu.VMEM((rows, HEAD_SIZE), f32),
            pltpu.VMEM((rows, HEAD_SIZE), f32),
            pltpu.VMEM((3, rows, HEAD_SIZE), f32),
            pltpu.VMEM((FFN_STEPS, rows, units), f32),
            pltpu.VMEM((FFN_STEPS, rows, units), f32),
            pltpu.VMEM((FFN_STEPS, rows, units), bf16),
            pltpu.VMEM((3, groups, rows, CHUNK), bf16),
            pltpu.VMEM((groups, rows, CHUNK), bf16),
            pltpu.VMEM((2, groups, rows, CHUNK), bf16),
            pltpu.VMEM((rows, width), bf16),
            pltpu.VMEM((rows, width), bf16),
            dma((7,)),
            dma,
            dma,
            dma((2, 3, pairs)),
            dma((2, 3, pairs)),
            dma((3, groups)),
            dma((3, groups)),
            dma((3,)),
            dma((3,)),
            dma((3, groups)),
            dma((3, groups)),
        ],
        compiler_params=pltpu.CompilerParams(
            collective_id=0, has_side_effects=True, vmem_limit_bytes=60 * 2**20
        ),
    )(q, k, v, positions.reshape(rows, 1), residual, gain.reshape(1, width), gate, up, down)


def solution(mesh):
    split = P("blk", None)
    in_specs = (split, split, split, P("blk"), split, P(), split, split, split)
    return jax.shard_map(
        functools.partial(per_device, mesh.shape["blk"]),
        mesh=mesh,
        in_specs=in_specs,
        out_specs=(split, split),
        check_vma=False,
    )
```

time: 391 us -> 210 us (0.54)
  Pallas kernels: 0 us -> 203 us
  waiting for transfers between devices: 161 us -> 0 us
  starting transfers between devices: 106 us -> 0 us
  matrix products: 82.8 us -> 0 us
  other arithmetic: 17.9 us -> 0 us
  local copies, waits for them, and re-layouts: 18.8 us -> 6.07 us
    pallas_call x0 -> x1, Pallas kernels: none -> 203 us  [per_device(): pl.pallas_call(functools.partial(layer_kernel, count), out_shape=(jax.Sha...]
    ppermute x12 -> x0, waiting for transfers between devices: 161 us -> none  [the longest x6 131 us: shifted(): return lax.ppermute(value, axis, pairs)]
    ppermute x12 -> x0, starting transfers between devices: 106 us -> none  [the longest x6 92.9 us: shifted(): return lax.ppermute(value, axis, pairs)]
    dot_general x24 -> x0, matrix products: 82.8 us -> none  [the longest x4 39 us: shard_term(): return jnp.dot(hidden, down_rows, preferred_element_type=jnp.float32)]
    reduce_sum x9 -> x0, other arithmetic: 9.71 us -> none  [the longest x8 7.21 us: group_of_head(): denominator = jnp.sum(weights, axis=-1, keepdims=True)]
    dynamic_slice x16 -> x0, local copies, waits for them, and re-layouts: 8.85 us -> none  [group_of_head(): lax.dynamic_slice_in_dim(query_states, group_index * heads_per_group * HE...]
    unnamed x15 -> x4, local copies, waits for them, and re-layouts: 9.57 us -> 4.6 us
    concatenate x2 -> x0, other arithmetic: 4.14 us -> none  [the longest x1 2.65 us: per_device(): jnp.concatenate([block_pair[1] for block_pair in ordered], axis=0)]
  transfers between devices with their start and end apart: 12 -> 0, of which waited for: 8 -> 0; matrix products, arithmetic and copies ran while one was open for 13% -> 0% of each run, Pallas kernels for 0% -> 0%
where the time goes in v2:
time: 210 us; the launch traced here: 209 us
  Pallas kernels  203 us (97%)
  local copies, waits for them, and re-layouts  6.07 us (3%)
    pallas_call x1, Pallas kernels, per_device(): pl.pallas_call(functools.partial(layer_kernel, count), out_shape=(jax.Sha...  203 us
    unnamed x4, local copies, waits for them, and re-layouts  4.6 us

profile of v2, /device:TPU:30, one launch (start us, length us, event | category | flops | bytes accessed | tf_op | source)
XLA Modules:
  0.0 209.5 jit_solution(12256185075742387203)
XLA Ops:
  0.6 1.5 copy.11.pos_ref
  2.1 202.8 %shard_map.104 = (bf16[256,4096]{1,0:T(8,128)(2,1)}, bf16[256,4096]{1,0:T(8,128)(2,1)}) custom-call(bf16[256,4096]{1,0:T(8,128)(2,1)} %q_hbm.1, bf16[256,1024]{1,0:T(8,128)(2,1)} %k_hbm.1, bf16[256,1024]{1,0:T(8,128)(2,1)} %v_hbm.1, s32[256,1]{1,0:T(8,128)} %copy.11.pos_ref, bf16[256,4096]{1,0:T(8,128)(2,1)} %res_hbm.1, f32[1,4096]{1,0:T(1,128)} %bitcast.2, ...), custom_call_target="tpu_custom_call" | custom-call | tf_op jit(solution)/shard_map/pallas_call | solution.py:345
  204.9 0.0 copy-start
  204.9 3.3 %copy.14 = bf16[256,4096]{1,0:T(8,128)(2,1)} copy(bf16[256,4096]{1,0:T(8,128)(2,1)} %get-tuple-element.4) | data formatting | bytes 4194304
  208.2 0.0 copy-done
  208.2 1.3 copy.15
Async XLA Ops:
  204.9 3.3 %copy-start = (bf16[256,4096]{1,0:T(8,128)(2,1)S(1)}, bf16[256,4096]{1,0:T(8,128)(2,1)}, u32[]{:S(2)}) copy-start(bf16[256,4096]{1,0:T(8,128)(2,1)} %get-tuple-element.5) | copy-start | bytes 6291460

commit v3 on v2

v3 whole, which is shorter than its diff:
```python
import functools
import math

import jax
import jax.numpy as jnp
from jax import lax
from jax.experimental import pallas as pl
from jax.experimental.pallas import tpu as pltpu
from jax.sharding import PartitionSpec as P

HEAD_SIZE = 128
KEY_VALUE_HEADS = 8
HEADS_PER_GROUP = 4
WINDOW_BLOCKS = 4
FFN_STEPS = 4
PAIR = 2 * HEAD_SIZE
CHUNK = HEADS_PER_GROUP * PAIR
TILES = 4
MESH = pl.DeviceIdType.MESH
NT = (((1,), (1,)), ((), ()))


def layer_kernel(
    count,
    q_hbm,
    k_hbm,
    v_hbm,
    pos_ref,
    res_hbm,
    gain_ref,
    gate_hbm,
    up_hbm,
    down_hbm,
    attended_hbm,
    ffn_hbm,
    q,
    k_own,
    v_own,
    res,
    gate,
    up,
    down,
    k_in,
    v_in,
    s_all,
    square,
    rs_all,
    acc_gate,
    acc_up,
    hidden,
    middle,
    own_total,
    part,
    x_in,
    r_in,
    att,
    ffn,
    load_sem,
    att_sem,
    ffn_sem,
    kv_send,
    kv_recv,
    s_send,
    s_recv,
    rs_send,
    rs_recv,
    p_send,
    p_recv,
):
    rows, width = q.shape
    pairs = KEY_VALUE_HEADS // 2
    tile = rows // TILES
    me = lax.axis_index("blk")
    core = lax.rem(me, 2)

    def at(offset):
        return lax.rem(me + offset + count, count)

    third, sibling = at(1 + 2 * core), at(1 - 2 * core)
    routes = ((at(2), 1, 0), (third, 2 * core, 2 + core), (sibling, 2 - 2 * core, 3 - core))

    loads = [
        pltpu.make_async_copy(src, dst, load_sem.at[i])
        for i, (src, dst) in enumerate(
            (
                (k_hbm, k_own),
                (v_hbm, v_own),
                (q_hbm, q),
                (res_hbm, res),
                (gate_hbm, gate),
                (up_hbm, up),
                (down_hbm, down),
            )
        )
    ]
    for load in loads:
        load.start()

    barrier = pltpu.get_barrier_semaphore()
    for offset in (1, 2, 3, -1, -2, -3):
        pl.semaphore_signal(barrier, inc=1, device_id=(at(offset),), device_id_type=MESH)
    pl.semaphore_wait(barrier, 6)

    def kv_copy(which, route, j):
        device, slot, _ = routes[route]
        own, arrived = ((k_hbm, k_in), (v_hbm, v_in))[which]
        if route == 2:
            src = arrived.at[1, j]
        else:
            src = own.at[:, pl.ds(pl.multiple_of(j * PAIR, PAIR), PAIR)]
        return pltpu.make_async_remote_copy(
            src_ref=src,
            dst_ref=arrived.at[slot, j],
            send_sem=kv_send.at[which, route, j],
            recv_sem=kv_recv.at[which, slot, j],
            device_id=(device,),
            device_id_type=MESH,
        )

    def kv_arrival(which, slot, j):
        arrived = (k_in, v_in)[which]
        pltpu.make_async_copy(arrived.at[slot, j], arrived.at[slot, j], kv_recv.at[which, slot, j]).wait()

    def s_copy(route, t, j):
        device, _, place = routes[route]
        return pltpu.make_async_remote_copy(
            src_ref=s_all.at[t, j, 0 if route == 2 else 1],
            dst_ref=s_all.at[t, j, place],
            send_sem=s_send.at[route, t, j],
            recv_sem=s_recv.at[place, t, j],
            device_id=(device,),
            device_id_type=MESH,
        )

    def s_arrival(place, t, j):
        here = s_all.at[t, j, place]
        pltpu.make_async_copy(here, here, s_recv.at[place, t, j]).wait()

    def rs_copy(route, t):
        device, _, place = routes[route]
        return pltpu.make_async_remote_copy(
            src_ref=rs_all.at[t, 0 if route == 2 else 1],
            dst_ref=rs_all.at[t, place],
            send_sem=rs_send.at[route, t],
            recv_sem=rs_recv.at[place, t],
            device_id=(device,),
            device_id_type=MESH,
        )

    def rs_arrival(place, t):
        here = rs_all.at[t, place]
        pltpu.make_async_copy(here, here, rs_recv.at[place, t]).wait()

    def p_landing(kind, t, j):
        return x_in.at[t, j] if kind == 0 else r_in.at[kind - 1, t, j]

    def p_copy(kind, t, j):
        return pltpu.make_async_remote_copy(
            src_ref=part.at[kind, t, j],
            dst_ref=p_landing(kind, t, j),
            send_sem=p_send.at[kind, t, j],
            recv_sem=p_recv.at[kind, t, j],
            device_id=((sibling, at(-2), at(2 * core - 3))[kind],),
            device_id_type=MESH,
        )

    def p_arrival(kind, t, j):
        here = p_landing(kind, t, j)
        pltpu.make_async_copy(here, here, p_recv.at[kind, t, j]).wait()

    def each(limit):
        def run(body):
            lax.fori_loop(0, limit, lambda i, c: (body(i), c)[1], 0)

        return run

    @each(pairs)
    def _(j):
        for which in range(2):
            for route in range(2):
                kv_copy(which, route, j).start()

    for load in loads[:4]:
        load.wait()

    factor = math.log2(math.e) / math.sqrt(HEAD_SIZE)
    row_ids = lax.broadcasted_iota(jnp.int32, (tile, rows), 0)
    column_ids = lax.broadcasted_iota(jnp.int32, (tile, rows), 1)

    def att_copy(t):
        here = pl.ds(pl.multiple_of(t * tile, tile), tile)
        return pltpu.make_async_copy(att.at[here], attended_hbm.at[here], att_sem.at[t])

    def ffn_copy(t):
        here = pl.ds(pl.multiple_of(t * tile, tile), tile)
        return pltpu.make_async_copy(ffn.at[here], ffn_hbm.at[here], ffn_sem.at[t])

    @each(TILES)
    def _(t):
        here = pl.ds(pl.multiple_of(t * tile, tile), tile)
        row = row_ids + t * tile
        first = row - pos_ref[here]
        bias = []
        for d in range(WINDOW_BLOCKS):
            key = column_ids - d * rows
            bias.append(jnp.where((key <= row) & (key >= first), 0.0, -jnp.inf))
        square[...] = jnp.zeros_like(square)

        @each(pairs)
        def _(j):
            @pl.when(t == 0)
            def _():
                for which in range(2):
                    kv_arrival(which, 1, j)
                    kv_copy(which, 2, j).start()
                for which in range(2):
                    kv_arrival(which, 0, j)
                    kv_arrival(which, 2, j)

            for half in range(2):
                inner = pl.ds(half * HEAD_SIZE, HEAD_SIZE)
                kv_cols = pl.ds(pl.multiple_of(j * PAIR + half * HEAD_SIZE, HEAD_SIZE), HEAD_SIZE)
                keys = [k_own[:, kv_cols]] + [k_in[s, j, :, inner] for s in range(3)]
                values = [v_own[:, kv_cols]] + [v_in[s, j, :, inner] for s in range(3)]
                starts = [(half * HEADS_PER_GROUP + h) * HEAD_SIZE for h in range(HEADS_PER_GROUP)]
                cols = [pl.ds(pl.multiple_of(j * CHUNK + at_, HEAD_SIZE), HEAD_SIZE) for at_ in starts]
                query = jnp.concatenate([q[here, c] for c in cols], axis=0)
                scores = []
                for d in range(WINDOW_BLOCKS):
                    score = lax.dot_general(query, keys[d], NT, preferred_element_type=jnp.float32)
                    score = score.reshape(HEADS_PER_GROUP, tile, rows) + bias[d][None]
                    scores.append(score.reshape(HEADS_PER_GROUP * tile, rows))
                top = functools.reduce(jnp.maximum, scores)
                top = jnp.max(top, axis=1, keepdims=True)
                weights = [jnp.exp2((score - top) * factor) for score in scores]
                total = jnp.sum(functools.reduce(jnp.add, weights), axis=1, keepdims=True)
                mixed = functools.reduce(
                    jnp.add,
                    [
                        jnp.dot(w.astype(jnp.bfloat16), v, preferred_element_type=jnp.float32)
                        for w, v in zip(weights, values)
                    ],
                )
                attended = (mixed / total).astype(jnp.bfloat16)
                for h in range(HEADS_PER_GROUP):
                    mine = attended[h * tile : (h + 1) * tile]
                    att[here, cols[h]] = mine
                    stream = res[here, cols[h]].astype(jnp.float32) + mine.astype(jnp.float32)
                    square[...] += stream * stream
                    s_all[t, j, 1, :, pl.ds(starts[h], HEAD_SIZE)] = (
                        stream * gain_ref[:, cols[h]]
                    ).astype(jnp.bfloat16)
            s_copy(0, t, j).start()
            s_copy(1, t, j).start()

        att_copy(t).start()
        mean = jnp.sum(square[...], axis=1, keepdims=True) * (1.0 / width)
        rs_all[t, 1] = jnp.broadcast_to(lax.rsqrt(mean + 1e-05), square.shape)
        rs_copy(0, t).start()
        rs_copy(1, t).start()

    for load in loads[4:]:
        load.wait()

    @each(TILES)
    def _(t):
        acc_gate[...] = jnp.zeros_like(acc_gate)
        acc_up[...] = jnp.zeros_like(acc_up)

        @each(pairs)
        def _(j):
            s_arrival(0, t, j)
            s_copy(2, t, j).start()

        rs_arrival(0, t)
        rs_copy(2, t).start()

        @each(pairs)
        def _(j):
            s_arrival(2, t, j)
            s_arrival(3, t, j)
            cols = pl.ds(pl.multiple_of(j * CHUNK, CHUNK), CHUNK)
            chunk = s_all[t, j].reshape(FFN_STEPS * tile, CHUNK)
            acc_gate[...] += lax.dot_general(chunk, gate[:, cols], NT, preferred_element_type=jnp.float32)
            acc_up[...] += lax.dot_general(chunk, up[:, cols], NT, preferred_element_type=jnp.float32)

        rs_arrival(2, t)
        rs_arrival(3, t)
        scale = rs_all[t].reshape(FFN_STEPS * tile, HEAD_SIZE)[:, :1]
        gate_value = acc_gate[...] * scale
        silu = gate_value / (1.0 + jnp.exp(-gate_value))
        hidden[...] = (silu * (acc_up[...] * scale)).astype(jnp.bfloat16).reshape(hidden.shape)

        @each(pairs)
        def _(j):
            cols = pl.ds(pl.multiple_of(j * CHUNK, CHUNK), CHUNK)
            fed = hidden[...].reshape(FFN_STEPS * tile, hidden.shape[2])
            sums = jnp.dot(fed, down[:, cols], preferred_element_type=jnp.float32)
            sums = sums.reshape(FFN_STEPS, tile, CHUNK)
            middle[j] = sums[0]
            own_total[t, j] = sums[1]
            even = core == 0
            part[0, t, j] = jnp.where(even, sums[2], sums[3]).astype(jnp.bfloat16)
            part[2, t, j] = jnp.where(even, sums[3], sums[2]).astype(jnp.bfloat16)
            p_copy(2, t, j).start()
            p_copy(0, t, j).start()

        @each(pairs)
        def _(j):
            p_arrival(0, t, j)
            part[1, t, j] = (middle[j] + x_in[t, j].astype(jnp.float32)).astype(jnp.bfloat16)
            p_copy(1, t, j).start()

    @each(TILES)
    def _(t):
        here = pl.ds(pl.multiple_of(t * tile, tile), tile)

        @each(pairs)
        def _(j):
            cols = pl.ds(pl.multiple_of(j * CHUNK, CHUNK), CHUNK)
            p_arrival(2, t, j)
            p_arrival(1, t, j)
            back = r_in[0, t, j].astype(jnp.float32) + r_in[1, t, j].astype(jnp.float32)
            ffn[here, cols] = (own_total[t, j] + back).astype(jnp.bfloat16)

        ffn_copy(t).start()

    @each(pairs)
    def _(j):
        for which in range(2):
            for route in range(3):
                kv_copy(which, route, j).wait_send()

    @each(TILES)
    def _(t):
        @each(pairs)
        def _(j):
            for route in range(3):
                s_copy(route, t, j).wait_send()
                p_copy(route, t, j).wait_send()

        for route in range(3):
            rs_copy(route, t).wait_send()
        att_copy(t).wait()
        ffn_copy(t).wait()


def per_device(count, q, k, v, positions, residual, gain, gate, up, down):
    rows, width = q.shape
    units = gate.shape[0]
    tile = rows // TILES
    pairs = KEY_VALUE_HEADS // 2
    bf16, f32 = jnp.bfloat16, jnp.float32
    any_spec = pl.BlockSpec(memory_space=pl.ANY)
    vmem_spec = pl.BlockSpec(memory_space=pltpu.VMEM)
    dma = pltpu.SemaphoreType.DMA
    return pl.pallas_call(
        functools.partial(layer_kernel, count),
        out_shape=(jax.ShapeDtypeStruct((rows, width), bf16),) * 2,
        in_specs=[any_spec, any_spec, any_spec, vmem_spec, any_spec, vmem_spec] + [any_spec] * 3,
        out_specs=(any_spec, any_spec),
        scratch_shapes=[
            pltpu.VMEM((rows, width), bf16),
            pltpu.VMEM(k.shape, bf16),
            pltpu.VMEM(v.shape, bf16),
            pltpu.VMEM((rows, width), bf16),
            pltpu.VMEM((units, width), bf16),
            pltpu.VMEM((units, width), bf16),
            pltpu.VMEM((units, width), bf16),
            pltpu.VMEM((3, pairs, rows, PAIR), bf16),
            pltpu.VMEM((3, pairs, rows, PAIR), bf16),
            pltpu.VMEM((TILES, pairs, FFN_STEPS, tile, CHUNK), bf16),
            pltpu.VMEM((tile, HEAD_SIZE), f32),
            pltpu.VMEM((TILES, FFN_STEPS, tile, HEAD_SIZE), f32),
            pltpu.VMEM((FFN_STEPS * tile, units), f32),
            pltpu.VMEM((FFN_STEPS * tile, units), f32),
            pltpu.VMEM((FFN_STEPS, tile, units), bf16),
            pltpu.VMEM((pairs, tile, CHUNK), f32),
            pltpu.VMEM((TILES, pairs, tile, CHUNK), f32),
            pltpu.VMEM((3, TILES, pairs, tile, CHUNK), bf16),
            pltpu.VMEM((TILES, pairs, tile, CHUNK), bf16),
            pltpu.VMEM((2, TILES, pairs, tile, CHUNK), bf16),
            pltpu.VMEM((rows, width), bf16),
            pltpu.VMEM((rows, width), bf16),
            dma((7,)),
            dma((TILES,)),
            dma((TILES,)),
            dma((2, 3, pairs)),
            dma((2, 3, pairs)),
            dma((3, TILES, pairs)),
            dma((4, TILES, pairs)),
            dma((3, TILES)),
            dma((4, TILES)),
            dma((3, TILES, pairs)),
            dma((3, TILES, pairs)),
        ],
        compiler_params=pltpu.CompilerParams(
            collective_id=0, has_side_effects=True, vmem_limit_bytes=60 * 2**20
        ),
    )(q, k, v, positions.reshape(rows, 1), residual, gain.reshape(1, width), gate, up, down)


def solution(mesh):
    split = P("blk", None)
    in_specs = (split, split, split, P("blk"), split, P(), split, split, split)
    return jax.shard_map(
        functools.partial(per_device, mesh.shape["blk"]),
        mesh=mesh,
        in_specs=in_specs,
        out_specs=(split, split),
        check_vma=False,
    )
```

time: 210 us -> 185 us (0.88)
  Pallas kernels: 203 us -> 178 us
    pallas_call x1, Pallas kernels: 203 us -> 178 us  [per_device(): pl.pallas_call(functools.partial(layer_kernel, count), out_shape=(jax.Sha...]
where the time goes in v3:
time: 185 us
  Pallas kernels  178 us (96%)
  local copies, waits for them, and re-layouts  6.07 us (3%)
    pallas_call x1, Pallas kernels, per_device(): pl.pallas_call(functools.partial(layer_kernel, count), out_shape=(jax.Sha...  178 us
    unnamed x4, local copies, waits for them, and re-layouts  4.6 us

profile of v3, /device:TPU:30, one launch (start us, length us, event | category | flops | bytes accessed | tf_op | source)
XLA Modules:
  0.0 184.8 jit_solution(3359410879067441050)
XLA Ops:
  0.6 1.5 copy.11.pos_ref
  2.1 178.1 %shard_map.104 = (bf16[256,4096]{1,0:T(8,128)(2,1)}, bf16[256,4096]{1,0:T(8,128)(2,1)}) custom-call(bf16[256,4096]{1,0:T(8,128)(2,1)} %q_hbm.1, bf16[256,1024]{1,0:T(8,128)(2,1)} %k_hbm.1, bf16[256,1024]{1,0:T(8,128)(2,1)} %v_hbm.1, s32[256,1]{1,0:T(8,128)} %copy.11.pos_ref, bf16[256,4096]{1,0:T(8,128)(2,1)} %res_hbm.1, f32[1,4096]{1,0:T(1,128)} %bitcast.2, ...), custom_call_target="tpu_custom_call" | custom-call | tf_op jit(solution)/shard_map/pallas_call | solution.py:357
  180.2 0.0 copy-start
  180.2 3.3 %copy.14 = bf16[256,4096]{1,0:T(8,128)(2,1)} copy(bf16[256,4096]{1,0:T(8,128)(2,1)} %get-tuple-element.4) | data formatting | bytes 4194304
  183.5 0.0 copy-done
  183.5 1.3 copy.15
Async XLA Ops:
  180.2 3.3 %copy-start = (bf16[256,4096]{1,0:T(8,128)(2,1)S(1)}, bf16[256,4096]{1,0:T(8,128)(2,1)}, u32[]{:S(2)}) copy-start(bf16[256,4096]{1,0:T(8,128)(2,1)} %get-tuple-element.5) | copy-start | bytes 6291460

commit v4 on v3

--- a/solution.py
+++ b/solution.py
@@ -43,6 +43,7 @@
     k_in,
     v_in,
     s_all,
+    first_key,
     square,
     rs_all,
     acc_gate,
@@ -174,11 +175,25 @@
 
         return run
 
-    @each(pairs)
-    def _(j):
-        for which in range(2):
-            for route in range(2):
-                kv_copy(which, route, j).start()
+    sends = (me + 2 < count, me + 1 + 2 * core < count)
+    reaches = (me >= 1, me >= 2, me >= 3)
+    forwards = reaches[1]
+
+    def kv_each(route, act):
+        @pl.when(forwards if route == 2 else sends[route])
+        def _():
+            @each(pairs)
+            def _(j):
+                for which in range(2):
+                    act(kv_copy(which, route, j))
+
+    for route in range(2):
+        kv_each(route, lambda copy: copy.start())
+    for slot in range(WINDOW_BLOCKS - 1):
+        @pl.when(jnp.logical_not(reaches[slot]))
+        def _():
+            k_in[slot] = jnp.zeros(k_in.shape[1:], k_in.dtype)
+            v_in[slot] = jnp.zeros(v_in.shape[1:], v_in.dtype)
 
     for load in loads[:4]:
         load.wait()
@@ -195,27 +210,44 @@
         here = pl.ds(pl.multiple_of(t * tile, tile), tile)
         return pltpu.make_async_copy(ffn.at[here], ffn_hbm.at[here], ffn_sem.at[t])
 
-    @each(TILES)
-    def _(t):
-        here = pl.ds(pl.multiple_of(t * tile, tile), tile)
-        row = row_ids + t * tile
-        first = row - pos_ref[here]
-        bias = []
-        for d in range(WINDOW_BLOCKS):
-            key = column_ids - d * rows
-            bias.append(jnp.where((key <= row) & (key >= first), 0.0, -jnp.inf))
-        square[...] = jnp.zeros_like(square)
-
-        @each(pairs)
-        def _(j):
-            @pl.when(t == 0)
+    diagonal = lax.broadcasted_iota(jnp.int32, (rows, rows), 0) - lax.broadcasted_iota(
+        jnp.int32, (rows, rows), 1
+    )
+    back = jnp.where(diagonal == 0, pos_ref[...].astype(jnp.float32), 0.0)
+    first_key[...] = (
+        lax.broadcasted_iota(jnp.int32, (rows, 1), 0).astype(jnp.float32)
+        - jnp.sum(back, axis=1, keepdims=True)
+    )
+    square[...] = jnp.zeros_like(square)
+
+    def send_rows(t, j):
+        s_copy(0, t, j).start()
+        s_copy(1, t, j).start()
+
+    @each(pairs)
+    def _(j):
+        @pl.when(reaches[1])
+        def _():
+            for which in range(2):
+                kv_arrival(which, 1, j)
+                kv_copy(which, 2, j).start()
+
+        for slot in (0, 2):
+            @pl.when(reaches[slot])
             def _():
                 for which in range(2):
-                    kv_arrival(which, 1, j)
-                    kv_copy(which, 2, j).start()
-                for which in range(2):
-                    kv_arrival(which, 0, j)
-                    kv_arrival(which, 2, j)
+                    kv_arrival(which, slot, j)
+
+        @each(TILES)
+        def _(t):
+            here = pl.ds(pl.multiple_of(t * tile, tile), tile)
+            row = row_ids + t * tile
+            first = first_key[here]
+            bias = []
+            for d in range(WINDOW_BLOCKS):
+                key = column_ids - d * rows
+                seen = (key <= row) & (key.astype(jnp.float32) >= first)
+                bias.append(jnp.where(seen, 0.0, -jnp.inf))
 
             for half in range(2):
                 inner = pl.ds(half * HEAD_SIZE, HEAD_SIZE)
@@ -246,18 +278,27 @@
                     mine = attended[h * tile : (h + 1) * tile]
                     att[here, cols[h]] = mine
                     stream = res[here, cols[h]].astype(jnp.float32) + mine.astype(jnp.float32)
-                    square[...] += stream * stream
+                    square[t] += stream * stream
                     s_all[t, j, 1, :, pl.ds(starts[h], HEAD_SIZE)] = (
                         stream * gain_ref[:, cols[h]]
                     ).astype(jnp.bfloat16)
-            s_copy(0, t, j).start()
-            s_copy(1, t, j).start()
-
-        att_copy(t).start()
-        mean = jnp.sum(square[...], axis=1, keepdims=True) * (1.0 / width)
-        rs_all[t, 1] = jnp.broadcast_to(lax.rsqrt(mean + 1e-05), square.shape)
-        rs_copy(0, t).start()
-        rs_copy(1, t).start()
+
+            @pl.when(t == 0)
+            def _():
+                send_rows(t, j)
+
+            @pl.when(j == pairs - 1)
+            def _():
+                @pl.when(t > 0)
+                def _():
+                    for earlier in range(pairs):
+                        send_rows(t, earlier)
+
+                mean = jnp.sum(square[t], axis=1, keepdims=True) * (1.0 / width)
+                rs_all[t, 1] = jnp.broadcast_to(lax.rsqrt(mean + 1e-05), rs_all.shape[2:])
+                rs_copy(0, t).start()
+                rs_copy(1, t).start()
+                att_copy(t).start()
 
     for load in loads[4:]:
         load.wait()
@@ -267,22 +308,23 @@
         acc_gate[...] = jnp.zeros_like(acc_gate)
         acc_up[...] = jnp.zeros_like(acc_up)
 
-        @each(pairs)
-        def _(j):
-            s_arrival(0, t, j)
-            s_copy(2, t, j).start()
-
-        rs_arrival(0, t)
-        rs_copy(2, t).start()
-
-        @each(pairs)
-        def _(j):
+        def add_chunk(j):
             s_arrival(2, t, j)
             s_arrival(3, t, j)
-            cols = pl.ds(pl.multiple_of(j * CHUNK, CHUNK), CHUNK)
+            cols = pl.ds(j * CHUNK, CHUNK)
             chunk = s_all[t, j].reshape(FFN_STEPS * tile, CHUNK)
             acc_gate[...] += lax.dot_general(chunk, gate[:, cols], NT, preferred_element_type=jnp.float32)
             acc_up[...] += lax.dot_general(chunk, up[:, cols], NT, preferred_element_type=jnp.float32)
+
+        for j in range(pairs):
+            s_arrival(0, t, j)
+            s_copy(2, t, j).start()
+            if j == pairs - 1:
+                rs_arrival(0, t)
+                rs_copy(2, t).start()
+            if j > 0:
+                add_chunk(j - 1)
+        add_chunk(pairs - 1)
 
         rs_arrival(2, t)
         rs_arrival(3, t)
@@ -291,25 +333,25 @@
         silu = gate_value / (1.0 + jnp.exp(-gate_value))
         hidden[...] = (silu * (acc_up[...] * scale)).astype(jnp.bfloat16).reshape(hidden.shape)
 
-        @each(pairs)
-        def _(j):
-            cols = pl.ds(pl.multiple_of(j * CHUNK, CHUNK), CHUNK)
+        def combine(j):
+            p_arrival(0, t, j)
+            part[1, t, j] = (middle[j] + x_in[t, j].astype(jnp.float32)).astype(jnp.bfloat16)
+            p_copy(1, t, j).start()
+
+        even = core == 0
+        for j in range(pairs):
             fed = hidden[...].reshape(FFN_STEPS * tile, hidden.shape[2])
-            sums = jnp.dot(fed, down[:, cols], preferred_element_type=jnp.float32)
+            sums = jnp.dot(fed, down[:, pl.ds(j * CHUNK, CHUNK)], preferred_element_type=jnp.float32)
             sums = sums.reshape(FFN_STEPS, tile, CHUNK)
             middle[j] = sums[0]
             own_total[t, j] = sums[1]
-            even = core == 0
             part[0, t, j] = jnp.where(even, sums[2], sums[3]).astype(jnp.bfloat16)
+            p_copy(0, t, j).start()
             part[2, t, j] = jnp.where(even, sums[3], sums[2]).astype(jnp.bfloat16)
             p_copy(2, t, j).start()
-            p_copy(0, t, j).start()
-
-        @each(pairs)
-        def _(j):
-            p_arrival(0, t, j)
-            part[1, t, j] = (middle[j] + x_in[t, j].astype(jnp.float32)).astype(jnp.bfloat16)
-            p_copy(1, t, j).start()
+            if j > 0:
+                combine(j - 1)
+        combine(pairs - 1)
 
     @each(TILES)
     def _(t):
@@ -325,11 +367,8 @@
 
         ffn_copy(t).start()
 
-    @each(pairs)
-    def _(j):
-        for which in range(2):
-            for route in range(3):
-                kv_copy(which, route, j).wait_send()
+    for route in range(3):
+        kv_each(route, lambda copy: copy.wait_send())
 
     @each(TILES)
     def _(t):
@@ -370,7 +409,8 @@
             pltpu.VMEM((3, pairs, rows, PAIR), bf16),
             pltpu.VMEM((3, pairs, rows, PAIR), bf16),
             pltpu.VMEM((TILES, pairs, FFN_STEPS, tile, CHUNK), bf16),
-            pltpu.VMEM((tile, HEAD_SIZE), f32),
+            pltpu.VMEM((rows, 1), f32),
+            pltpu.VMEM((TILES, tile, HEAD_SIZE), f32),
             pltpu.VMEM((TILES, FFN_STEPS, tile, HEAD_SIZE), f32),
             pltpu.VMEM((FFN_STEPS * tile, units), f32),
             pltpu.VMEM((FFN_STEPS * tile, units), f32),
@@ -397,7 +437,7 @@
         compiler_params=pltpu.CompilerParams(
             collective_id=0, has_side_effects=True, vmem_limit_bytes=60 * 2**20
         ),
-    )(q, k, v, positions.reshape(rows, 1), residual, gain.reshape(1, width), gate, up, down)
+    )(q, k, v, positions.reshape(1, rows), residual, gain.reshape(1, width), gate, up, down)
 
 
 def solution(mesh):

time: 185 us -> 198 us (1.070)
  the two profiles are of different devices: /device:TPU:30 before, /device:TPU:3 now
where the time goes in v4:
time: 198 us
  Pallas kernels  192 us (97%)
  local copies, waits for them, and re-layouts  4.6 us (2%)
    pallas_call x1, Pallas kernels, per_device(): pl.pallas_call(functools.partial(layer_kernel, count), out_shape=(jax.Sha...  192 us
    unnamed x4, local copies, waits for them, and re-layouts  4.6 us

profile of v4, /device:TPU:3, one launch (start us, length us, event | category | flops | bytes accessed | tf_op | source)
XLA Modules:
  0.0 197.7 jit_solution(9639468182298535086)
XLA Ops:
  0.6 192.5 %shard_map.104 = (bf16[256,4096]{1,0:T(8,128)(2,1)}, bf16[256,4096]{1,0:T(8,128)(2,1)}) custom-call(bf16[256,4096]{1,0:T(8,128)(2,1)} %q_hbm.1, bf16[256,1024]{1,0:T(8,128)(2,1)} %k_hbm.1, bf16[256,1024]{1,0:T(8,128)(2,1)} %v_hbm.1, s32[1,256]{1,0:T(1,128)} %bitcast.3, bf16[256,4096]{1,0:T(8,128)(2,1)} %res_hbm.1, f32[1,4096]{1,0:T(1,128)} %bitcast.2, ...), custom_call_target="tpu_custom_call" | custom-call | tf_op jit(solution)/shard_map/pallas_call | solution.py:396
  193.1 0.0 copy-start
  193.1 3.3 %copy.13 = bf16[256,4096]{1,0:T(8,128)(2,1)} copy(bf16[256,4096]{1,0:T(8,128)(2,1)} %get-tuple-element.4) | data formatting | bytes 4194304
  196.4 0.0 copy-done
  196.4 1.3 copy.14
Async XLA Ops:
  193.1 3.3 %copy-start = (bf16[256,4096]{1,0:T(8,128)(2,1)S(1)}, bf16[256,4096]{1,0:T(8,128)(2,1)}, u32[]{:S(2)}) copy-start(bf16[256,4096]{1,0:T(8,128)(2,1)} %get-tuple-element.5) | copy-start | bytes 6291460

commit v5 on v4

--- a/solution.py
+++ b/solution.py
@@ -224,30 +224,31 @@
         s_copy(0, t, j).start()
         s_copy(1, t, j).start()
 
-    @each(pairs)
-    def _(j):
-        @pl.when(reaches[1])
-        def _():
-            for which in range(2):
-                kv_arrival(which, 1, j)
-                kv_copy(which, 2, j).start()
-
-        for slot in (0, 2):
-            @pl.when(reaches[slot])
-            def _():
-                for which in range(2):
-                    kv_arrival(which, slot, j)
-
-        @each(TILES)
-        def _(t):
-            here = pl.ds(pl.multiple_of(t * tile, tile), tile)
-            row = row_ids + t * tile
-            first = first_key[here]
-            bias = []
-            for d in range(WINDOW_BLOCKS):
-                key = column_ids - d * rows
-                seen = (key <= row) & (key.astype(jnp.float32) >= first)
-                bias.append(jnp.where(seen, 0.0, -jnp.inf))
+    def attend(t, first_tile=False):
+        here = pl.ds(pl.multiple_of(t * tile, tile), tile)
+        row = row_ids + t * tile
+        first = first_key[here]
+        bias = []
+        for d in range(WINDOW_BLOCKS):
+            key = column_ids - d * rows
+            seen = (key <= row) & (key.astype(jnp.float32) >= first)
+            bias.append(jnp.where(seen, 0.0, -jnp.inf))
+
+
+        @each(pairs)
+        def _(j):
+            if first_tile:
+                @pl.when(reaches[1])
+                def _():
+                    for which in range(2):
+                        kv_arrival(which, 1, j)
+                        kv_copy(which, 2, j).start()
+
+                for slot in (0, 2):
+                    @pl.when(reaches[slot])
+                    def _():
+                        for which in range(2):
+                            kv_arrival(which, slot, j)
 
             for half in range(2):
                 inner = pl.ds(half * HEAD_SIZE, HEAD_SIZE)
@@ -282,29 +283,24 @@
                     s_all[t, j, 1, :, pl.ds(starts[h], HEAD_SIZE)] = (
                         stream * gain_ref[:, cols[h]]
                     ).astype(jnp.bfloat16)
-
-            @pl.when(t == 0)
-            def _():
-                send_rows(t, j)
-
-            @pl.when(j == pairs - 1)
-            def _():
-                @pl.when(t > 0)
-                def _():
-                    for earlier in range(pairs):
-                        send_rows(t, earlier)
-
-                mean = jnp.sum(square[t], axis=1, keepdims=True) * (1.0 / width)
-                rs_all[t, 1] = jnp.broadcast_to(lax.rsqrt(mean + 1e-05), rs_all.shape[2:])
-                rs_copy(0, t).start()
-                rs_copy(1, t).start()
-                att_copy(t).start()
-
+            send_rows(t, j)
+
+        mean = jnp.sum(square[t], axis=1, keepdims=True) * (1.0 / width)
+        rs_all[t, 1] = jnp.broadcast_to(lax.rsqrt(mean + 1e-05), rs_all.shape[2:])
+        rs_copy(0, t).start()
+        rs_copy(1, t).start()
+        att_copy(t).start()
+
+    attend(0, first_tile=True)
     for load in loads[4:]:
         load.wait()
 
     @each(TILES)
     def _(t):
+        @pl.when(t + 1 < TILES)
+        def _():
+            attend(t + 1)
+
         acc_gate[...] = jnp.zeros_like(acc_gate)
         acc_up[...] = jnp.zeros_like(acc_up)
 

time: 198 us -> 186 us (0.939)
  the two profiles are of different devices: /device:TPU:3 before, /device:TPU:21 now
where the time goes in v5:
time: 186 us
  Pallas kernels  181 us (97%)
  local copies, waits for them, and re-layouts  4.6 us (2%)
    pallas_call x1, Pallas kernels, per_device(): pl.pallas_call(functools.partial(layer_kernel, count), out_shape=(jax.Sha...  181 us
    unnamed x4, local copies, waits for them, and re-layouts  4.6 us

profile of v5, /device:TPU:21, one launch (start us, length us, event | category | flops | bytes accessed | tf_op | source)
XLA Modules:
  0.0 186.1 jit_solution(1610064744544217602)
XLA Ops:
  0.6 180.8 %shard_map.104 = (bf16[256,4096]{1,0:T(8,128)(2,1)}, bf16[256,4096]{1,0:T(8,128)(2,1)}) custom-call(bf16[256,4096]{1,0:T(8,128)(2,1)} %q_hbm.1, bf16[256,1024]{1,0:T(8,128)(2,1)} %k_hbm.1, bf16[256,1024]{1,0:T(8,128)(2,1)} %v_hbm.1, s32[1,256]{1,0:T(1,128)} %bitcast.3, bf16[256,4096]{1,0:T(8,128)(2,1)} %res_hbm.1, f32[1,4096]{1,0:T(1,128)} %bitcast.2, ...), custom_call_target="tpu_custom_call" | custom-call | tf_op jit(solution)/shard_map/pallas_call | solution.py:392
  181.5 0.0 copy-start
  181.5 3.3 %copy.13 = bf16[256,4096]{1,0:T(8,128)(2,1)} copy(bf16[256,4096]{1,0:T(8,128)(2,1)} %get-tuple-element.4) | data formatting | bytes 4194304
  184.8 0.0 copy-done
  184.8 1.3 copy.14
Async XLA Ops:
  181.5 3.3 %copy-start = (bf16[256,4096]{1,0:T(8,128)(2,1)S(1)}, bf16[256,4096]{1,0:T(8,128)(2,1)}, u32[]{:S(2)}) copy-start(bf16[256,4096]{1,0:T(8,128)(2,1)} %get-tuple-element.5) | copy-start | bytes 6291460

commit v6 on v5

--- a/solution.py
+++ b/solution.py
@@ -78,7 +78,16 @@
         return lax.rem(me + offset + count, count)
 
     third, sibling = at(1 + 2 * core), at(1 - 2 * core)
-    routes = ((at(2), 1, 0), (third, 2 * core, 2 + core), (sibling, 2 - 2 * core, 3 - core))
+    odd_chip = lax.rem(lax.div(me, 2), 2) == 1
+    direct = jnp.logical_not(odd_chip & (core == 1))
+    relay = odd_chip & (core == 0)
+    routes = (
+        (at(2), 1, 0),
+        (third, 2 * core, 2 + core),
+        (sibling, 2 - 2 * core, 3 - core),
+        (at(-1), 1, 0),
+    )
+    source_place = (1, 1, 0, 3)
 
     loads = [
         pltpu.make_async_copy(src, dst, load_sem.at[i])
@@ -105,8 +114,8 @@
     def kv_copy(which, route, j):
         device, slot, _ = routes[route]
         own, arrived = ((k_hbm, k_in), (v_hbm, v_in))[which]
-        if route == 2:
-            src = arrived.at[1, j]
+        if route >= 2:
+            src = arrived.at[route - 1, j]
         else:
             src = own.at[:, pl.ds(pl.multiple_of(j * PAIR, PAIR), PAIR)]
         return pltpu.make_async_remote_copy(
@@ -125,7 +134,7 @@
     def s_copy(route, t, j):
         device, _, place = routes[route]
         return pltpu.make_async_remote_copy(
-            src_ref=s_all.at[t, j, 0 if route == 2 else 1],
+            src_ref=s_all.at[t, j, source_place[route]],
             dst_ref=s_all.at[t, j, place],
             send_sem=s_send.at[route, t, j],
             recv_sem=s_recv.at[place, t, j],
@@ -140,7 +149,7 @@
     def rs_copy(route, t):
         device, _, place = routes[route]
         return pltpu.make_async_remote_copy(
-            src_ref=rs_all.at[t, 0 if route == 2 else 1],
+            src_ref=rs_all.at[t, source_place[route]],
             dst_ref=rs_all.at[t, place],
             send_sem=rs_send.at[route, t],
             recv_sem=rs_recv.at[place, t],
@@ -175,12 +184,16 @@
 
         return run
 
-    sends = (me + 2 < count, me + 1 + 2 * core < count)
     reaches = (me >= 1, me >= 2, me >= 3)
-    forwards = reaches[1]
+    sends = (
+        direct & (me + 2 < count),
+        me + 1 + 2 * core < count,
+        reaches[1],
+        relay & reaches[2],
+    )
 
     def kv_each(route, act):
-        @pl.when(forwards if route == 2 else sends[route])
+        @pl.when(sends[route])
         def _():
             @each(pairs)
             def _(j):
@@ -221,7 +234,10 @@
     square[...] = jnp.zeros_like(square)
 
     def send_rows(t, j):
-        s_copy(0, t, j).start()
+        @pl.when(direct)
+        def _():
+            s_copy(0, t, j).start()
+
         s_copy(1, t, j).start()
 
     def attend(t, first_tile=False):
@@ -238,14 +254,22 @@
         @each(pairs)
         def _(j):
             if first_tile:
+                @pl.when(reaches[2])
+                def _():
+                    @pl.when(relay)
+                    def _():
+                        for which in range(2):
+                            kv_arrival(which, 2, j)
+                            kv_copy(which, 3, j).start()
+
                 @pl.when(reaches[1])
                 def _():
                     for which in range(2):
                         kv_arrival(which, 1, j)
                         kv_copy(which, 2, j).start()
 
-                for slot in (0, 2):
-                    @pl.when(reaches[slot])
+                for slot, waits in ((0, reaches[0]), (2, reaches[2] & jnp.logical_not(relay))):
+                    @pl.when(waits)
                     def _():
                         for which in range(2):
                             kv_arrival(which, slot, j)
@@ -287,7 +311,10 @@
 
         mean = jnp.sum(square[t], axis=1, keepdims=True) * (1.0 / width)
         rs_all[t, 1] = jnp.broadcast_to(lax.rsqrt(mean + 1e-05), rs_all.shape[2:])
-        rs_copy(0, t).start()
+        @pl.when(direct)
+        def _():
+            rs_copy(0, t).start()
+
         rs_copy(1, t).start()
         att_copy(t).start()
 
@@ -306,13 +333,25 @@
 
         def add_chunk(j):
             s_arrival(2, t, j)
-            s_arrival(3, t, j)
+
+            @pl.when(jnp.logical_not(relay))
+            def _():
+                s_arrival(3, t, j)
+
             cols = pl.ds(j * CHUNK, CHUNK)
             chunk = s_all[t, j].reshape(FFN_STEPS * tile, CHUNK)
             acc_gate[...] += lax.dot_general(chunk, gate[:, cols], NT, preferred_element_type=jnp.float32)
             acc_up[...] += lax.dot_general(chunk, up[:, cols], NT, preferred_element_type=jnp.float32)
 
         for j in range(pairs):
+            @pl.when(relay)
+            def _():
+                s_arrival(3, t, j)
+                s_copy(3, t, j).start()
+                if j == pairs - 1:
+                    rs_arrival(3, t)
+                    rs_copy(3, t).start()
+
             s_arrival(0, t, j)
             s_copy(2, t, j).start()
             if j == pairs - 1:
@@ -323,7 +362,11 @@
         add_chunk(pairs - 1)
 
         rs_arrival(2, t)
-        rs_arrival(3, t)
+
+        @pl.when(jnp.logical_not(relay))
+        def _():
+            rs_arrival(3, t)
+
         scale = rs_all[t].reshape(FFN_STEPS * tile, HEAD_SIZE)[:, :1]
         gate_value = acc_gate[...] * scale
         silu = gate_value / (1.0 + jnp.exp(-gate_value))
@@ -363,19 +406,29 @@
 
         ffn_copy(t).start()
 
-    for route in range(3):
+    for route in range(4):
         kv_each(route, lambda copy: copy.wait_send())
 
     @each(TILES)
     def _(t):
+        for route, started in ((0, direct), (1, None), (2, None), (3, relay)):
+            def finish(route=route):
+                rs_copy(route, t).wait_send()
+
+                @each(pairs)
+                def _(j):
+                    s_copy(route, t, j).wait_send()
+
+            if started is None:
+                finish()
+            else:
+                pl.when(started)(finish)
+
         @each(pairs)
         def _(j):
-            for route in range(3):
-                s_copy(route, t, j).wait_send()
-                p_copy(route, t, j).wait_send()
-
-        for route in range(3):
-            rs_copy(route, t).wait_send()
+            for kind in range(3):
+                p_copy(kind, t, j).wait_send()
+
         att_copy(t).wait()
         ffn_copy(t).wait()
 
@@ -421,11 +474,11 @@
             dma((7,)),
             dma((TILES,)),
             dma((TILES,)),
+            dma((2, 4, pairs)),
             dma((2, 3, pairs)),
-            dma((2, 3, pairs)),
-            dma((3, TILES, pairs)),
             dma((4, TILES, pairs)),
-            dma((3, TILES)),
+            dma((4, TILES, pairs)),
+            dma((4, TILES)),
             dma((4, TILES)),
             dma((3, TILES, pairs)),
             dma((3, TILES, pairs)),

time: 186 us -> 153 us (0.82)
  the two profiles are of different devices: /device:TPU:21 before, /device:TPU:30 now
where the time goes in v6:
time: 153 us; the launch traced here: 152 us
  Pallas kernels  147 us (96%)
  local copies, waits for them, and re-layouts  4.6 us (3%)
    pallas_call x1, Pallas kernels, per_device(): pl.pallas_call(functools.partial(layer_kernel, count), out_shape=(jax.Sha...  147 us
    unnamed x4, local copies, waits for them, and re-layouts  4.6 us

profile of v6, /device:TPU:30, one launch (start us, length us, event | category | flops | bytes accessed | tf_op | source)
XLA Modules:
  0.0 152.2 jit_solution(15015717031900202319)
XLA Ops:
  0.6 147.0 %shard_map.104 = (bf16[256,4096]{1,0:T(8,128)(2,1)}, bf16[256,4096]{1,0:T(8,128)(2,1)}) custom-call(bf16[256,4096]{1,0:T(8,128)(2,1)} %q_hbm.1, bf16[256,1024]{1,0:T(8,128)(2,1)} %k_hbm.1, bf16[256,1024]{1,0:T(8,128)(2,1)} %v_hbm.1, s32[1,256]{1,0:T(1,128)} %bitcast.3, bf16[256,4096]{1,0:T(8,128)(2,1)} %res_hbm.1, f32[1,4096]{1,0:T(1,128)} %bitcast.2, ...), custom_call_target="tpu_custom_call" | custom-call | tf_op jit(solution)/shard_map/pallas_call | solution.py:445
  147.6 0.0 copy-start
  147.6 3.3 %copy.13 = bf16[256,4096]{1,0:T(8,128)(2,1)} copy(bf16[256,4096]{1,0:T(8,128)(2,1)} %get-tuple-element.4) | data formatting | bytes 4194304
  150.9 0.0 copy-done
  150.9 1.3 copy.14
Async XLA Ops:
  147.6 3.3 %copy-start = (bf16[256,4096]{1,0:T(8,128)(2,1)S(1)}, bf16[256,4096]{1,0:T(8,128)(2,1)}, u32[]{:S(2)}) copy-start(bf16[256,4096]{1,0:T(8,128)(2,1)} %get-tuple-element.5) | copy-start | bytes 6291460

commit v7 on v6

--- a/solution.py
+++ b/solution.py
@@ -53,6 +53,8 @@
     own_total,
     part,
     x_in,
+    y_in,
+    late,
     r_in,
     att,
     ffn,
@@ -81,6 +83,7 @@
     odd_chip = lax.rem(lax.div(me, 2), 2) == 1
     direct = jnp.logical_not(odd_chip & (core == 1))
     relay = odd_chip & (core == 0)
+    hands_on = jnp.logical_not(odd_chip) & (core == 1)
     routes = (
         (at(2), 1, 0),
         (third, 2 * core, 2 + core),
@@ -162,15 +165,17 @@
         pltpu.make_async_copy(here, here, rs_recv.at[place, t]).wait()
 
     def p_landing(kind, t, j):
+        if kind == 3:
+            return y_in.at[t, j]
         return x_in.at[t, j] if kind == 0 else r_in.at[kind - 1, t, j]
 
     def p_copy(kind, t, j):
         return pltpu.make_async_remote_copy(
-            src_ref=part.at[kind, t, j],
+            src_ref=part.at[1 if kind == 3 else kind, t, j],
             dst_ref=p_landing(kind, t, j),
             send_sem=p_send.at[kind, t, j],
             recv_sem=p_recv.at[kind, t, j],
-            device_id=((sibling, at(-2), at(2 * core - 3))[kind],),
+            device_id=((sibling, at(-2), at(2 * core - 3), at(1))[kind],),
             device_id_type=MESH,
         )
 
@@ -375,7 +380,14 @@
         def combine(j):
             p_arrival(0, t, j)
             part[1, t, j] = (middle[j] + x_in[t, j].astype(jnp.float32)).astype(jnp.bfloat16)
-            p_copy(1, t, j).start()
+
+            @pl.when(hands_on)
+            def _():
+                p_copy(3, t, j).start()
+
+            @pl.when(jnp.logical_not(hands_on))
+            def _():
+                p_copy(1, t, j).start()
 
         even = core == 0
         for j in range(pairs):
@@ -386,11 +398,24 @@
             own_total[t, j] = sums[1]
             part[0, t, j] = jnp.where(even, sums[2], sums[3]).astype(jnp.bfloat16)
             p_copy(0, t, j).start()
-            part[2, t, j] = jnp.where(even, sums[3], sums[2]).astype(jnp.bfloat16)
-            p_copy(2, t, j).start()
+            late[j] = jnp.where(even, sums[3], sums[2])
+
+            @pl.when(jnp.logical_not(relay))
+            def _():
+                part[2, t, j] = late[j].astype(jnp.bfloat16)
+                p_copy(2, t, j).start()
+
             if j > 0:
                 combine(j - 1)
         combine(pairs - 1)
+
+        @pl.when(relay)
+        def _():
+            @each(pairs)
+            def _(j):
+                p_arrival(3, t, j)
+                part[2, t, j] = (late[j] + y_in[t, j].astype(jnp.float32)).astype(jnp.bfloat16)
+                p_copy(2, t, j).start()
 
     @each(TILES)
     def _(t):
@@ -400,9 +425,14 @@
         def _(j):
             cols = pl.ds(pl.multiple_of(j * CHUNK, CHUNK), CHUNK)
             p_arrival(2, t, j)
-            p_arrival(1, t, j)
-            back = r_in[0, t, j].astype(jnp.float32) + r_in[1, t, j].astype(jnp.float32)
-            ffn[here, cols] = (own_total[t, j] + back).astype(jnp.bfloat16)
+            own_total[t, j] += r_in[1, t, j].astype(jnp.float32)
+
+            @pl.when(direct)
+            def _():
+                p_arrival(1, t, j)
+                own_total[t, j] += r_in[0, t, j].astype(jnp.float32)
+
+            ffn[here, cols] = own_total[t, j].astype(jnp.bfloat16)
 
         ffn_copy(t).start()
 
@@ -426,8 +456,16 @@
 
         @each(pairs)
         def _(j):
-            for kind in range(3):
-                p_copy(kind, t, j).wait_send()
+            p_copy(0, t, j).wait_send()
+            p_copy(2, t, j).wait_send()
+
+            @pl.when(hands_on)
+            def _():
+                p_copy(3, t, j).wait_send()
+
+            @pl.when(jnp.logical_not(hands_on))
+            def _():
+                p_copy(1, t, j).wait_send()
 
         att_copy(t).wait()
         ffn_copy(t).wait()
@@ -468,6 +506,8 @@
             pltpu.VMEM((TILES, pairs, tile, CHUNK), f32),
             pltpu.VMEM((3, TILES, pairs, tile, CHUNK), bf16),
             pltpu.VMEM((TILES, pairs, tile, CHUNK), bf16),
+            pltpu.VMEM((TILES, pairs, tile, CHUNK), bf16),
+            pltpu.VMEM((pairs, tile, CHUNK), f32),
             pltpu.VMEM((2, TILES, pairs, tile, CHUNK), bf16),
             pltpu.VMEM((rows, width), bf16),
             pltpu.VMEM((rows, width), bf16),
@@ -480,8 +520,8 @@
             dma((4, TILES, pairs)),
             dma((4, TILES)),
             dma((4, TILES)),
-            dma((3, TILES, pairs)),
-            dma((3, TILES, pairs)),
+            dma((4, TILES, pairs)),
+            dma((4, TILES, pairs)),
         ],
         compiler_params=pltpu.CompilerParams(
             collective_id=0, has_side_effects=True, vmem_limit_bytes=60 * 2**20

time: 153 us -> 176 us (1.15); the launches traced: 152 us -> 173 us
  Pallas kernels: 147 us -> 168 us
    pallas_call x1, Pallas kernels: 147 us -> 168 us  [per_device(): pl.pallas_call(functools.partial(layer_kernel, count), out_shape=(jax.Sha...]
where the time goes in v7:
time: 176 us; the launch traced here: 173 us
  Pallas kernels  168 us (95%)
  local copies, waits for them, and re-layouts  4.6 us (3%)
    pallas_call x1, Pallas kernels, per_device(): pl.pallas_call(functools.partial(layer_kernel, count), out_shape=(jax.Sha...  168 us
    unnamed x4, local copies, waits for them, and re-layouts  4.6 us

profile of v7, /device:TPU:30, one launch (start us, length us, event | category | flops | bytes accessed | tf_op | source)
XLA Modules:
  0.0 173.4 jit_solution(7321435391567960794)
XLA Ops:
  0.6 168.1 %shard_map.104 = (bf16[256,4096]{1,0:T(8,128)(2,1)}, bf16[256,4096]{1,0:T(8,128)(2,1)}) custom-call(bf16[256,4096]{1,0:T(8,128)(2,1)} %q_hbm.1, bf16[256,1024]{1,0:T(8,128)(2,1)} %k_hbm.1, bf16[256,1024]{1,0:T(8,128)(2,1)} %v_hbm.1, s32[1,256]{1,0:T(1,128)} %bitcast.3, bf16[256,4096]{1,0:T(8,128)(2,1)} %res_hbm.1, f32[1,4096]{1,0:T(1,128)} %bitcast.2, ...), custom_call_target="tpu_custom_call" | custom-call | tf_op jit(solution)/shard_map/pallas_call | solution.py:483
  168.7 0.0 copy-start
  168.8 3.3 %copy.13 = bf16[256,4096]{1,0:T(8,128)(2,1)} copy(bf16[256,4096]{1,0:T(8,128)(2,1)} %get-tuple-element.4) | data formatting | bytes 4194304
  172.0 0.0 copy-done
  172.0 1.3 copy.14
Async XLA Ops:
  168.7 3.3 %copy-start = (bf16[256,4096]{1,0:T(8,128)(2,1)S(1)}, bf16[256,4096]{1,0:T(8,128)(2,1)}, u32[]{:S(2)}) copy-start(bf16[256,4096]{1,0:T(8,128)(2,1)} %get-tuple-element.5) | copy-start | bytes 6291460
